TPU v7x, 32 devices: a whole 2x2x4 slice. The times are simulated.
32 devices in a mesh: band: 8 (over y, x, core), tile: 4 (over z).
Axes of the slice: x: 2, y: 2, z: 4, core: 2. Of those that a mesh axis runs over, the one named last changes fastest.
Arguments:
- coarse_source: float32 [128, 512], P('band', 'tile'), may hold values from 0.1 to 10
- coarse_target: float32 [128, 512], P('band', 'tile'), may hold values from 0.1 to 10
- target_offset: float32 [1024, 128], P(('band', 'tile')), may hold values from -4 to 122, as said below
- source_mass: float32 [1024, 128], P(('band', 'tile')), may hold values from 0.003 to 10
- target_mass: float32 [1024, 128], P(('band', 'tile')), may hold values from 0.1 to 10
- cell_count: int32 [1024], P(('band', 'tile')), may hold values from 1 to 128
- pair_source: int32 [16384], P(('band', 'tile')), may hold values from 0 to 32, as said below
- pair_target: int32 [16384], P(('band', 'tile')), may hold values from 0 to 1023, as said below
Outputs:
- scaling_u: float32 [128, 512], P('band', 'tile')
- scaling_v: float32 [128, 512], P('band', 'tile')
- source_potential: float32 [1024, 128], P(('band', 'tile'))
- target_potential: float32 [1024, 128], P(('band', 'tile'))
Inputs may be any that keep to these rules, and one draw needn't show every extreme that they name: `target_offset`: A float of order one in each cell; in some tiles it may carry a large common level. `pair_source`: on each device, slot l < 32 is live with local source tile l; every local source tile appears; the live slots come first on each device, the others hold 32; on some device all 512 slots are live. `pair_target`: A live slot of slot index l < 32 on device d targets tile d * 32 + l; any live slot targets a tile of its device's band or an adjacent band, in any longitude block; an unused slot holds its device's first tile.
All inputs are finite; a program needn't handle non-finite values.
Results may differ from a plain program's by a relative error of at most 0.000075.
Values sent between devices are 32-bit elements; how exact they have to be, the bound alone decides.
A program may use at most 64 MiB of HBM per device.

v0:
```python
import math

import jax
import jax.numpy as jnp
from jax import lax
from jax.sharding import PartitionSpec as P

COARSE_ITERS = 2


entropy = 0.5
damping = 0.8
coarse_power = 0.8
kernel_taps = [math.exp(-0.125 * offset * offset) for offset in range(-4, 5)]


def with_halo(block, sides, width):
    for axis, dim in sides:
        count = lax.axis_size(axis)
        forward = [(i, i + 1) for i in range(count - 1)]
        backward = [(target, source) for source, target in forward]
        low = lax.ppermute(
            lax.slice_in_dim(block, block.shape[dim] - width, None, axis=dim), axis, forward
        )
        high = lax.ppermute(lax.slice_in_dim(block, 0, width, axis=dim), axis, backward)
        block = jnp.concatenate([low, block, high], axis=dim)
    return block


def passed_along(value, axis, steps):
    count = lax.axis_size(axis)
    leading, last = (max(0, -steps), min(count, count - steps))
    return lax.ppermute(value, axis, [(source, source + steps) for source in range(leading, last)])


def blur(padded, rows, cols):
    across = kernel_taps[0] * padded[0:rows, :]
    for offset in range(1, 9):
        across = across + kernel_taps[offset] * padded[offset : offset + rows, :]
    result = kernel_taps[0] * across[:, 0:cols]
    for offset in range(1, 9):
        result = result + kernel_taps[offset] * across[:, offset : offset + cols]
    return result


def combine(first, second):
    peak = jnp.maximum(first[0], second[0])
    safe = jnp.where(peak == -jnp.inf, jnp.float32(0.0), peak)
    return (peak, first[1] * jnp.exp(first[0] - safe) + second[1] * jnp.exp(second[0] - safe))


def per_device(
    coarse_source,
    coarse_target,
    target_offset,
    source_mass,
    target_mass,
    cell_count,
    pair_source,
    pair_target,
):
    rows, cols = coarse_source.shape

    def smooth(field):
        padded = with_halo(field, (("band", 0), ("tile", 1)), 4)
        return blur(padded, rows, cols)

    scaling_v = jnp.ones_like(coarse_target)
    scaling_u = scaling_v
    for step in range(COARSE_ITERS):
        scaling_u = (coarse_source / smooth(scaling_v)) ** coarse_power
        scaling_v = (coarse_target / smooth(scaling_u)) ** coarse_power
    tiles_here, width = target_offset.shape
    parent = jnp.repeat(jnp.log(scaling_v), tiles_here // rows, axis=0)
    target_field = (target_offset + entropy * parent) / entropy + jnp.log(target_mass)
    band = lax.axis_index("band")
    column = lax.axis_index("tile")
    n_band = lax.axis_size("band")
    n_tile = lax.axis_size("tile")
    full_cols = n_tile * width
    cost_unit = float(full_cols * full_cols) / 4.0
    scale = cost_unit * entropy
    cell = jnp.arange(width, dtype=jnp.int32).astype(jnp.float32)
    mixing = jnp.exp(2.0 * cell[:, None] * cell[None, :] / scale)
    band_tiles = n_tile * tiles_here
    target_device = pair_target // tiles_here
    rimmed = with_halo(target_field.reshape(1, tiles_here, width), (("band", 0),), 1)
    window = lax.all_gather(rimmed, "tile", axis=1, tiled=True).reshape(3 * band_tiles, width)
    where_window = pair_target - (band - 1) * band_tiles
    slots = pair_source.shape[0]
    block = math.gcd(slots, 128)
    valid = pair_source < tiles_here
    source_local = jnp.minimum(pair_source, tiles_here - 1)
    tgt_row = (target_device // n_tile * tiles_here + pair_target % tiles_here).astype(jnp.float32)
    tgt_col = (target_device % n_tile * width).astype(jnp.float32)
    src_row = (band * tiles_here + source_local).astype(jnp.float32)
    src_col = (column * width).astype(jnp.float32)
    drow = (src_row - tgt_row).reshape(-1, block)
    dcol = (src_col - tgt_col).reshape(-1, block)
    neg = jnp.float32(-jnp.inf)

    def row_block(inputs):
        part_row, part_col, fields = inputs
        lifted = (
            fields
            - (cell * cell)[None, :] / scale
            + 2.0 * part_col[:, None] * cell[None, :] / scale
        )
        high = jnp.max(lifted, axis=1)
        total = jnp.dot(
            jnp.exp(lifted - high[:, None]),
            mixing,
            precision=lax.Precision.HIGHEST,
            preferred_element_type=jnp.float32,
        )
        shifted = part_col[:, None] + cell[None, :]
        top = high[:, None] - (part_row[:, None] * part_row[:, None] + shifted * shifted) / scale
        return (top, total)

    def col_block(inputs):
        part_row, part_col, fields = inputs
        lifted = (
            fields
            - (cell * cell)[None, :] / scale
            - 2.0 * part_col[:, None] * cell[None, :] / scale
        )
        high = jnp.max(lifted, axis=1)
        total = jnp.dot(
            jnp.exp(lifted - high[:, None]),
            mixing,
            precision=lax.Precision.HIGHEST,
            preferred_element_type=jnp.float32,
        )
        shifted = part_col[:, None] - cell[None, :]
        top = high[:, None] - (part_row[:, None] * part_row[:, None] + shifted * shifted) / scale
        return (top, total)

    tops, totals = lax.map(row_block, (drow, dcol, window[where_window].reshape(-1, block, width)))
    tops = tops.reshape(slots, width)
    totals = totals.reshape(slots, width)
    peak = (
        jnp.full((tiles_here, width), neg, jnp.float32)
        .at[source_local]
        .max(jnp.where(valid[:, None], tops, neg))
    )
    weighted = jnp.where(
        valid[:, None], totals * jnp.exp(tops - peak[source_local]), jnp.float32(0.0)
    )
    summed = jnp.zeros((tiles_here, width), jnp.float32).at[source_local].add(weighted)
    source_potential = -damping * entropy * (peak + jnp.log(summed))
    active = jnp.arange(width, dtype=jnp.int32)[None, :] < cell_count[:, None]
    source_field = jnp.where(active, source_potential / entropy + jnp.log(source_mass), neg)
    tops, totals = lax.map(
        col_block, (drow, dcol, source_field[source_local].reshape(-1, block, width))
    )
    tops = tops.reshape(slots, width)
    totals = totals.reshape(slots, width)
    window_tiles = window.shape[0]
    win_peak = (
        jnp.full((window_tiles, width), neg, jnp.float32)
        .at[where_window]
        .max(jnp.where(valid[:, None], tops, neg))
    )
    safe_peak = jnp.where(win_peak == -jnp.inf, jnp.float32(0.0), win_peak)
    weighted = jnp.where(
        valid[:, None], totals * jnp.exp(tops - safe_peak[where_window]), jnp.float32(0.0)
    )
    win_total = jnp.zeros((window_tiles, width), jnp.float32).at[where_window].add(weighted)
    peak_three = win_peak.reshape(3, band_tiles, width)
    total_three = win_total.reshape(3, band_tiles, width)
    top_three = lax.pmax(peak_three, "tile")
    scaled = jnp.where(
        peak_three == -jnp.inf, jnp.float32(0.0), total_three * jnp.exp(peak_three - top_three)
    )
    share_total = lax.psum_scatter(scaled, "tile", scatter_dimension=1, tiled=True)
    share_peak = lax.dynamic_slice_in_dim(top_three, column * tiles_here, tiles_here, 1)
    from_above = passed_along((share_peak[0], share_total[0]), "band", -1)
    from_below = passed_along((share_peak[2], share_total[2]), "band", 1)
    above_peak = jnp.where(band == n_band - 1, neg, from_above[0])
    below_peak = jnp.where(band == 0, neg, from_below[0])
    middle = (share_peak[1], share_total[1])
    own_peak, own_total = combine(
        combine(middle, (above_peak, from_above[1])), (below_peak, from_below[1])
    )
    target_potential = -damping * entropy * (own_peak + jnp.log(own_total))
    return (scaling_u, scaling_v, source_potential, target_potential)


def solution(mesh):
    placed = (
        P("band", "tile"),
        P("band", "tile"),
        P(("band", "tile"), None),
        P(("band", "tile"), None),
        P(("band", "tile"), None),
        P(("band", "tile")),
        P(("band", "tile")),
        P(("band", "tile")),
    )
    return jax.shard_map(
        per_device,
        mesh=mesh,
        in_specs=placed,
        out_specs=(
            P("band", "tile"),
            P("band", "tile"),
            P(("band", "tile"), None),
            P(("band", "tile"), None),
        ),
        check_vma=False,
    )
```

profile of v0, /device:TPU:3, one launch (start us, length us, event | category | flops | bytes accessed | tf_op | source)
XLA Modules:
  0.0 192.0 jit_solution(14216488098353721993)
XLA Ops:
  7.2 2.6 %collective-permute-start.1 = (f32[4,128]{1,0:T(4,128)S(1)}, f32[4,128]{1,0:T(4,128)S(1)}, u32[]{:S(2)}, u32[]{:S(2)}) collective-permute-start(f32[4,128]{1,0:T(4,128)S(1)} %broadcast.328), channel_id=1, source_target_pairs={{4,0},{8,4},{12,8},{16,12},{20,16},{24,20},{28,24},{5,1},{9,5},{13... | collective-permute-start | bytes 6152 | tf_op jit(solution)/shard_map/ppermute | solution.py:25
  9.8 3.9 %collective-permute-start = (f32[4,128]{1,0:T(4,128)S(1)}, f32[4,128]{1,0:T(4,128)S(1)}, u32[]{:S(2)}, u32[]{:S(2)}) collective-permute-start(f32[4,128]{1,0:T(4,128)S(1)} %broadcast.328), channel_id=1, source_target_pairs={{0,4},{4,8},{8,12},{12,16},{16,20},{20,24},{24,28},{1,5},{5,9},{9,... | collective-permute-start | bytes 6152 | tf_op jit(solution)/shard_map/ppermute | solution.py:22
  14.5 1.4 collective-permute-start.3
  15.9 4.0 %collective-permute-start.2 = (f32[24,4]{1,0:T(8,128)S(1)}, f32[24,4]{1,0:T(8,128)S(1)}, u32[]{:S(2)}, u32[]{:S(2)}) collective-permute-start(f32[24,4]{1,0:T(8,128)S(1)} %get-tuple-element.312), channel_id=1, source_target_pairs={{0,1},{1,2},{2,3},{4,5},{5,6},{6,7},{8,9},{9,10},{10,11},{12,13},{... | collective-permute-start | bytes 1160 | tf_op jit(solution)/shard_map/ppermute | solution.py:22
  21.6 3.4 %collective-permute-start.5 = (f32[4,128]{1,0:T(4,128)S(1)}, f32[4,128]{1,0:T(4,128)S(1)}, u32[]{:S(2)}, u32[]{:S(2)}) collective-permute-start(f32[4,128]{1,0:T(4,128)S(1)} %get-tuple-element.319), channel_id=1, source_target_pairs={{4,0},{8,4},{12,8},{16,12},{20,16},{24,20},{28,24},{5,1},{9,5},{13... | collective-permute-start | bytes 6152 | tf_op jit(solution)/shard_map/ppermute | solution.py:25
  25.0 4.8 %collective-permute-start.4 = (f32[4,128]{1,0:T(4,128)S(1)}, f32[4,128]{1,0:T(4,128)S(1)}, u32[]{:S(2)}, u32[]{:S(2)}) collective-permute-start(f32[4,128]{1,0:T(4,128)S(1)} %get-tuple-element.318), channel_id=1, source_target_pairs={{0,4},{4,8},{8,12},{12,16},{16,20},{20,24},{24,28},{1,5},{5,9},{9,... | collective-permute-start | bytes 6152 | tf_op jit(solution)/shard_map/ppermute | solution.py:22
  30.6 1.3 collective-permute-start.7
  31.9 4.5 %collective-permute-start.6 = (f32[24,4]{1,0:T(8,128)S(1)}, f32[24,4]{1,0:T(8,128)S(1)}, u32[]{:S(2)}, u32[]{:S(2)}) collective-permute-start(f32[24,4]{1,0:T(8,128)S(1)} %get-tuple-element.310), channel_id=1, source_target_pairs={{0,1},{1,2},{2,3},{4,5},{5,6},{6,7},{8,9},{9,10},{10,11},{12,13},{... | collective-permute-start | bytes 1160 | tf_op jit(solution)/shard_map/ppermute | solution.py:22
  38.2 2.2 %collective-permute-start.9 = (f32[4,128]{1,0:T(4,128)S(1)}, f32[4,128]{1,0:T(4,128)S(1)}, u32[]{:S(2)}, u32[]{:S(2)}) collective-permute-start(f32[4,128]{1,0:T(4,128)S(1)} %get-tuple-element.317), channel_id=1, source_target_pairs={{4,0},{8,4},{12,8},{16,12},{20,16},{24,20},{28,24},{5,1},{9,5},{13... | collective-permute-start | bytes 6152 | tf_op jit(solution)/shard_map/ppermute | solution.py:25
  40.3 5.7 %collective-permute-start.8 = (f32[4,128]{1,0:T(4,128)S(1)}, f32[4,128]{1,0:T(4,128)S(1)}, u32[]{:S(2)}, u32[]{:S(2)}) collective-permute-start(f32[4,128]{1,0:T(4,128)S(1)} %get-tuple-element.316), channel_id=1, source_target_pairs={{0,4},{4,8},{8,12},{12,16},{16,20},{20,24},{24,28},{1,5},{5,9},{9,... | collective-permute-start | bytes 6152 | tf_op jit(solution)/shard_map/ppermute | solution.py:22
  48.1 4.5 %collective-permute-start.10 = (f32[24,4]{1,0:T(8,128)S(1)}, f32[24,4]{1,0:T(8,128)S(1)}, u32[]{:S(2)}, u32[]{:S(2)}) collective-permute-start(f32[24,4]{1,0:T(8,128)S(1)} %get-tuple-element.308), channel_id=1, source_target_pairs={{0,1},{1,2},{2,3},{4,5},{5,6},{6,7},{8,9},{9,10},{10,11},{12,13},{... | collective-permute-start | bytes 1160 | tf_op jit(solution)/shard_map/ppermute | solution.py:22
  53.7 1.9 %collective-permute-start.13 = (f32[4,128]{1,0:T(4,128)S(1)}, f32[4,128]{1,0:T(4,128)S(1)}, u32[]{:S(2)}, u32[]{:S(2)}) collective-permute-start(f32[4,128]{1,0:T(4,128)S(1)} %get-tuple-element.315), channel_id=1, source_target_pairs={{4,0},{8,4},{12,8},{16,12},{20,16},{24,20},{28,24},{5,1},{9,5},{13... | collective-permute-start | bytes 6152 | tf_op jit(solution)/shard_map/ppermute | solution.py:25
  55.6 5.9 %collective-permute-start.12 = (f32[4,128]{1,0:T(4,128)S(1)}, f32[4,128]{1,0:T(4,128)S(1)}, u32[]{:S(2)}, u32[]{:S(2)}) collective-permute-start(f32[4,128]{1,0:T(4,128)S(1)} %get-tuple-element.314), channel_id=1, source_target_pairs={{0,4},{4,8},{8,12},{12,16},{16,20},{20,24},{24,28},{1,5},{5,9},{9,... | collective-permute-start | bytes 6152 | tf_op jit(solution)/shard_map/ppermute | solution.py:22
  63.7 4.5 %collective-permute-start.14 = (f32[24,4]{1,0:T(8,128)S(1)}, f32[24,4]{1,0:T(8,128)S(1)}, u32[]{:S(2)}, u32[]{:S(2)}) collective-permute-start(f32[24,4]{1,0:T(8,128)S(1)} %get-tuple-element.306), channel_id=1, source_target_pairs={{0,1},{1,2},{2,3},{4,5},{5,6},{6,7},{8,9},{9,10},{10,11},{12,13},{... | collective-permute-start | bytes 1160 | tf_op jit(solution)/shard_map/ppermute | solution.py:22
  70.0 1.9 %collective-permute-start.17 = (f32[1,32,128]{2,1,0:T(8,128)S(1)}, f32[1,32,128]{2,1,0:T(8,128)S(1)}, u32[]{:S(2)}, u32[]{:S(2)}) collective-permute-start(f32[1,32,128]{2,1,0:T(8,128)S(1)} %add_bitcast_fusion), channel_id=1, source_target_pairs={{4,0},{8,4},{12,8},{16,12},{20,16},{24,20},{28,24},{5,1},{9,5},{13... | collective-permute-start | bytes 49160 | tf_op jit(solution)/shard_map/ppermute | solution.py:25
  71.9 5.9 %collective-permute-start.16 = (f32[1,32,128]{2,1,0:T(8,128)S(1)}, f32[1,32,128]{2,1,0:T(8,128)S(1)}, u32[]{:S(2)}, u32[]{:S(2)}) collective-permute-start(f32[1,32,128]{2,1,0:T(8,128)S(1)} %add_bitcast_fusion), channel_id=1, source_target_pairs={{0,4},{4,8},{8,12},{12,16},{16,20},{20,24},{24,28},{1,5},{5,9},{9,... | collective-permute-start | bytes 49160 | tf_op jit(solution)/shard_map/ppermute | solution.py:22
  78.7 12.5 %all_gather.3 = f32[3,128,128]{2,1,0:T(8,128)S(1)} all-gather(f32[3,32,128]{2,1,0:T(8,128)S(1)} %pad_maximum_fusion), channel_id=1, replica_groups=mesh['band'=8,'tile'=4] {'tile'}, dimensions={1}, use_global_device_ids=true | all-gather | bytes 245760 | tf_op jit(solution)/shard_map/all_gather | solution.py:88
  92.3 2.7 %while.30 = (s32[]{:T(128)}, f32[4,128,128]{2,1,0:T(8,128)S(1)}, f32[4,128,128]{2,1,0:T(8,128)S(1)}, f32[4,128,128]{2,1,0:T(8,128)S(1)}, f32[4,128]{1,0:T(4,128)...) while((s32[]{:T(128)}, f32[4,128,128]{2,1,0:T(8,128)S(1)}, ...), condition=%wide.region_2.3_spmd.clone.clone, body=%wide.region_0.2_spmd.clone.clone.sunk | while | flops 25444992 | bytes 274037 | solution.py:138
  95.2 3.5 %scatter_custom_fusion = f32[32,128]{1,0:T(8,128)S(1)} fusion(s32[512]{0:T(512)S(1)} %compare_select_fusion.4, f32[512,128]{1,0:T(8,128)S(1)} %bitcast_select_fusion.1, f32[]{:T(128)} %constant.153.clone.1), kind=kCustom, calls=%fused_computation.255 | custom fusion | flops 65536 | bytes 16388 | tf_op jit(solution)/shard_map/scatter-max | solution.py:144
  99.9 3.5 %scatter_custom_fusion.1 = f32[32,128]{1,0:T(8,128)S(1)} fusion(s32[512]{0:T(512)S(1)} %compare_select_fusion.4, f32[512,128]{1,0:T(8,128)S(1)} %fusion.58, f32[]{:T(128)} %constant.157.clone.1), kind=kCustom, calls=%fused_computation.252 | custom fusion | flops 65536 | bytes 16388 | tf_op jit(solution)/shard_map/scatter-add | solution.py:149
  105.2 2.7 %while.31 = (s32[]{:T(128)}, f32[4,128,128]{2,1,0:T(8,128)S(1)}, f32[4,128,128]{2,1,0:T(8,128)S(1)}, f32[4,128,128]{2,1,0:T(8,128)S(1)}, f32[4,128]{1,0:T(4,128)...) while((s32[]{:T(128)}, f32[4,128,128]{2,1,0:T(8,128)S(1)}, ...), condition=%wide.region_7.8_spmd.clone.clone, body=%wide.region_5.7_spmd.clone.clone.sunk | while | flops 25444992 | bytes 274037 | solution.py:153
  108.0 3.6 %scatter_custom_fusion.2 = f32[384,128]{1,0:T(8,128)S(1)} fusion(s32[512]{0:T(512)S(1)} %compare_select_fusion.3, f32[512,128]{1,0:T(8,128)S(1)} %bitcast_select_fusion, f32[]{:T(128)} %constant.153.clone.1), kind=kCustom, calls=%fused_computation.86 | custom fusion | flops 65536 | bytes 196612 | tf_op jit(solution)/shard_map/scatter-max | solution.py:162
  113.6 3.6 %scatter_custom_fusion.3 = f32[384,128]{1,0:T(8,128)S(1)} fusion(s32[512]{0:T(512)S(1)} %compare_select_fusion.3, f32[512,128]{1,0:T(8,128)S(1)} %fusion.56, f32[]{:T(128)} %constant.157.clone.1), kind=kCustom, calls=%fused_computation.84 | custom fusion | flops 65536 | bytes 196612 | tf_op jit(solution)/shard_map/scatter-add | solution.py:168
  117.1 33.2 %all-reduce.2.cloned.1.call-done = f32[3,128,128]{2,1,0:T(8,128)} async-done(((f32[3,128,128]{2,1,0:T(8,128)}), f32[3,128,128]{2,1,0:T(8,128)}) %all-reduce.2.cloned.1.call-update) | async-done | bytes 196624 | tf_op jit(solution)/shard_map/pmax | solution.py:171
  150.3 1.6 multiply_select_fusion
  152.7 5.5 %collective-permute-start.19 = (f32[32,128]{1,0:T(8,128)S(1)}, f32[32,128]{1,0:T(8,128)S(1)}, u32[]{:S(2)}, u32[]{:S(2)}) collective-permute-start(f32[32,128]{1,0:T(8,128)S(1)} %get-tuple-element.301), channel_id=1, source_target_pairs={{0,4},{4,8},{8,12},{12,16},{16,20},{20,24},{24,28},{1,5},{5,9},{9,... | collective-permute-start | bytes 49160 | tf_op jit(solution)/shard_map/ppermute | solution.py:33
  158.2 1.9 %collective-permute-start.18 = (f32[32,128]{1,0:T(8,128)S(1)}, f32[32,128]{1,0:T(8,128)S(1)}, u32[]{:S(2)}, u32[]{:S(2)}) collective-permute-start(f32[32,128]{1,0:T(8,128)S(1)} %get-tuple-element.300), channel_id=1, source_target_pairs={{4,0},{8,4},{12,8},{16,12},{20,16},{24,20},{28,24},{5,1},{9,5},{13... | collective-permute-start | bytes 49160 | tf_op jit(solution)/shard_map/ppermute | solution.py:33
  160.1 11.1 %reduce-scatter.2.cloned.1.call-done = f32[3,32,128]{2,1,0:T(8,128)} async-done(((f32[3,128,128]{2,1,0:T(8,128)}), f32[3,32,128]{2,1,0:T(8,128)}) %reduce-scatter.2.cloned.1.call-update) | async-done | bytes 49168 | tf_op jit(solution)/shard_map/reduce_scatter | solution.py:175
  172.0 5.8 %collective-permute-start.21 = (f32[32,128]{1,0:T(8,128)S(1)}, f32[32,128]{1,0:T(8,128)S(1)}, u32[]{:S(2)}, u32[]{:S(2)}) collective-permute-start(f32[32,128]{1,0:T(8,128)S(1)} %get-tuple-element.303), channel_id=1, source_target_pairs={{0,4},{4,8},{8,12},{12,16},{16,20},{20,24},{24,28},{1,5},{5,9},{9,... | collective-permute-start | bytes 49160 | tf_op jit(solution)/shard_map/ppermute | solution.py:33
  177.8 1.9 %collective-permute-start.20 = (f32[32,128]{1,0:T(8,128)S(1)}, f32[32,128]{1,0:T(8,128)S(1)}, u32[]{:S(2)}, u32[]{:S(2)}) collective-permute-start(f32[32,128]{1,0:T(8,128)S(1)} %get-tuple-element.302), channel_id=1, source_target_pairs={{4,0},{8,4},{12,8},{16,12},{20,16},{24,20},{28,24},{5,1},{9,5},{13... | collective-permute-start | bytes 49160 | tf_op jit(solution)/shard_map/ppermute | solution.py:33
  180.4 3.4 %collective-permute-done.20 = f32[32,128]{1,0:T(8,128)S(1)} collective-permute-done((f32[32,128]{1,0:T(8,128)S(1)}, f32[32,128]{1,0:T(8,128)S(1)}, u32[]{:S(2)}, u32[]{:S(2)}) %collective-permute-start.20) | collective-permute-done | bytes 16416 | tf_op jit(solution)/shard_map/ppermute | solution.py:33
  183.8 1.4 fusion.70
  (158 shorter events, 25.8 us)
Async XLA Ops:
  7.2 143.1 %all-reduce.2.cloned.1.call-start = ((), (), s32[]{:S(2)}) async-start(), calls=%async_computation.1 | async-start | bytes 393216 | tf_op jit(solution)/shard_map/pmax | solution.py:171
  7.2 6.5 %collective-permute-start.1 = (f32[4,128]{1,0:T(4,128)S(1)}, f32[4,128]{1,0:T(4,128)S(1)}, u32[]{:S(2)}, u32[]{:S(2)}) collective-permute-start(f32[4,128]{1,0:T(4,128)S(1)} %broadcast.328), channel_id=1, source_target_pairs={{4,0},{8,4},{12,8},{16,12},{20,16},{24,20},{28,24},{5,1},{9,5},{13... | collective-permute-start | bytes 6152 | tf_op jit(solution)/shard_map/ppermute | solution.py:25
  9.8 4.6 %collective-permute-start = (f32[4,128]{1,0:T(4,128)S(1)}, f32[4,128]{1,0:T(4,128)S(1)}, u32[]{:S(2)}, u32[]{:S(2)}) collective-permute-start(f32[4,128]{1,0:T(4,128)S(1)} %broadcast.328), channel_id=1, source_target_pairs={{0,4},{4,8},{8,12},{12,16},{16,20},{20,24},{24,28},{1,5},{5,9},{9,... | collective-permute-start | bytes 6152 | tf_op jit(solution)/shard_map/ppermute | solution.py:22
  14.4 5.5 %copy-start.9 = (s32[512]{0:T(512)S(1)}, s32[512]{0:T(512)}, u32[]{:S(2)}) copy-start(s32[512]{0:T(512)} %param.19) | copy-start | bytes 6148
  14.5 5.4 %copy-start.5 = (s32[512]{0:T(512)S(1)}, s32[512]{0:T(512)}, u32[]{:S(2)}) copy-start(s32[512]{0:T(512)} %param.18) | copy-start | bytes 6148
  14.5 5.5 %collective-permute-start.3 = (f32[24,4]{1,0:T(8,128)S(1)}, f32[24,4]{1,0:T(8,128)S(1)}, u32[]{:S(2)}, u32[]{:S(2)}) collective-permute-start(f32[24,4]{1,0:T(8,128)S(1)} %get-tuple-element.313), channel_id=1, source_target_pairs={{1,0},{2,1},{3,2},{5,4},{6,5},{7,6},{9,8},{10,9},{11,10},{13,12},{... | collective-permute-start | bytes 1160 | tf_op jit(solution)/shard_map/ppermute | solution.py:25
  15.9 4.8 %collective-permute-start.2 = (f32[24,4]{1,0:T(8,128)S(1)}, f32[24,4]{1,0:T(8,128)S(1)}, u32[]{:S(2)}, u32[]{:S(2)}) collective-permute-start(f32[24,4]{1,0:T(8,128)S(1)} %get-tuple-element.312), channel_id=1, source_target_pairs={{0,1},{1,2},{2,3},{4,5},{5,6},{6,7},{8,9},{9,10},{10,11},{12,13},{... | collective-permute-start | bytes 1160 | tf_op jit(solution)/shard_map/ppermute | solution.py:22
  21.6 8.2 %collective-permute-start.5 = (f32[4,128]{1,0:T(4,128)S(1)}, f32[4,128]{1,0:T(4,128)S(1)}, u32[]{:S(2)}, u32[]{:S(2)}) collective-permute-start(f32[4,128]{1,0:T(4,128)S(1)} %get-tuple-element.319), channel_id=1, source_target_pairs={{4,0},{8,4},{12,8},{16,12},{20,16},{24,20},{28,24},{5,1},{9,5},{13... | collective-permute-start | bytes 6152 | tf_op jit(solution)/shard_map/ppermute | solution.py:25
  25.0 5.5 %collective-permute-start.4 = (f32[4,128]{1,0:T(4,128)S(1)}, f32[4,128]{1,0:T(4,128)S(1)}, u32[]{:S(2)}, u32[]{:S(2)}) collective-permute-start(f32[4,128]{1,0:T(4,128)S(1)} %get-tuple-element.318), channel_id=1, source_target_pairs={{0,4},{4,8},{8,12},{12,16},{16,20},{20,24},{24,28},{1,5},{5,9},{9,... | collective-permute-start | bytes 6152 | tf_op jit(solution)/shard_map/ppermute | solution.py:22
  30.6 5.9 %collective-permute-start.7 = (f32[24,4]{1,0:T(8,128)S(1)}, f32[24,4]{1,0:T(8,128)S(1)}, u32[]{:S(2)}, u32[]{:S(2)}) collective-permute-start(f32[24,4]{1,0:T(8,128)S(1)} %get-tuple-element.311), channel_id=1, source_target_pairs={{1,0},{2,1},{3,2},{5,4},{6,5},{7,6},{9,8},{10,9},{11,10},{13,12},{... | collective-permute-start | bytes 1160 | tf_op jit(solution)/shard_map/ppermute | solution.py:25
  31.9 5.4 %collective-permute-start.6 = (f32[24,4]{1,0:T(8,128)S(1)}, f32[24,4]{1,0:T(8,128)S(1)}, u32[]{:S(2)}, u32[]{:S(2)}) collective-permute-start(f32[24,4]{1,0:T(8,128)S(1)} %get-tuple-element.310), channel_id=1, source_target_pairs={{0,1},{1,2},{2,3},{4,5},{5,6},{6,7},{8,9},{9,10},{10,11},{12,13},{... | collective-permute-start | bytes 1160 | tf_op jit(solution)/shard_map/ppermute | solution.py:22
  38.2 7.9 %collective-permute-start.9 = (f32[4,128]{1,0:T(4,128)S(1)}, f32[4,128]{1,0:T(4,128)S(1)}, u32[]{:S(2)}, u32[]{:S(2)}) collective-permute-start(f32[4,128]{1,0:T(4,128)S(1)} %get-tuple-element.317), channel_id=1, source_target_pairs={{4,0},{8,4},{12,8},{16,12},{20,16},{24,20},{28,24},{5,1},{9,5},{13... | collective-permute-start | bytes 6152 | tf_op jit(solution)/shard_map/ppermute | solution.py:25
  40.3 6.4 %collective-permute-start.8 = (f32[4,128]{1,0:T(4,128)S(1)}, f32[4,128]{1,0:T(4,128)S(1)}, u32[]{:S(2)}, u32[]{:S(2)}) collective-permute-start(f32[4,128]{1,0:T(4,128)S(1)} %get-tuple-element.316), channel_id=1, source_target_pairs={{0,4},{4,8},{8,12},{12,16},{16,20},{20,24},{24,28},{1,5},{5,9},{9,... | collective-permute-start | bytes 6152 | tf_op jit(solution)/shard_map/ppermute | solution.py:22
  46.8 5.9 %collective-permute-start.11 = (f32[24,4]{1,0:T(8,128)S(1)}, f32[24,4]{1,0:T(8,128)S(1)}, u32[]{:S(2)}, u32[]{:S(2)}) collective-permute-start(f32[24,4]{1,0:T(8,128)S(1)} %get-tuple-element.309), channel_id=1, source_target_pairs={{1,0},{2,1},{3,2},{5,4},{6,5},{7,6},{9,8},{10,9},{11,10},{13,12},{... | collective-permute-start | bytes 1160 | tf_op jit(solution)/shard_map/ppermute | solution.py:25
  48.1 5.4 %collective-permute-start.10 = (f32[24,4]{1,0:T(8,128)S(1)}, f32[24,4]{1,0:T(8,128)S(1)}, u32[]{:S(2)}, u32[]{:S(2)}) collective-permute-start(f32[24,4]{1,0:T(8,128)S(1)} %get-tuple-element.308), channel_id=1, source_target_pairs={{0,1},{1,2},{2,3},{4,5},{5,6},{6,7},{8,9},{9,10},{10,11},{12,13},{... | collective-permute-start | bytes 1160 | tf_op jit(solution)/shard_map/ppermute | solution.py:22
  53.7 15.4 %copy-start.2 = (f32[16,128]{1,0:T(8,128)}, f32[16,128]{1,0:T(8,128)S(1)}, u32[]{:S(2)}) copy-start(f32[16,128]{1,0:T(8,128)S(1)} %fusion.109) | copy-start | bytes 24580
  53.7 7.9 %collective-permute-start.13 = (f32[4,128]{1,0:T(4,128)S(1)}, f32[4,128]{1,0:T(4,128)S(1)}, u32[]{:S(2)}, u32[]{:S(2)}) collective-permute-start(f32[4,128]{1,0:T(4,128)S(1)} %get-tuple-element.315), channel_id=1, source_target_pairs={{4,0},{8,4},{12,8},{16,12},{20,16},{24,20},{28,24},{5,1},{9,5},{13... | collective-permute-start | bytes 6152 | tf_op jit(solution)/shard_map/ppermute | solution.py:25
  55.6 6.7 %collective-permute-start.12 = (f32[4,128]{1,0:T(4,128)S(1)}, f32[4,128]{1,0:T(4,128)S(1)}, u32[]{:S(2)}, u32[]{:S(2)}) collective-permute-start(f32[4,128]{1,0:T(4,128)S(1)} %get-tuple-element.314), channel_id=1, source_target_pairs={{0,4},{4,8},{8,12},{12,16},{16,20},{20,24},{24,28},{1,5},{5,9},{9,... | collective-permute-start | bytes 6152 | tf_op jit(solution)/shard_map/ppermute | solution.py:22
  62.4 5.9 %collective-permute-start.15 = (f32[24,4]{1,0:T(8,128)S(1)}, f32[24,4]{1,0:T(8,128)S(1)}, u32[]{:S(2)}, u32[]{:S(2)}) collective-permute-start(f32[24,4]{1,0:T(8,128)S(1)} %get-tuple-element.307), channel_id=1, source_target_pairs={{1,0},{2,1},{3,2},{5,4},{6,5},{7,6},{9,8},{10,9},{11,10},{13,12},{... | collective-permute-start | bytes 1160 | tf_op jit(solution)/shard_map/ppermute | solution.py:25
  63.7 5.4 %collective-permute-start.14 = (f32[24,4]{1,0:T(8,128)S(1)}, f32[24,4]{1,0:T(8,128)S(1)}, u32[]{:S(2)}, u32[]{:S(2)}) collective-permute-start(f32[24,4]{1,0:T(8,128)S(1)} %get-tuple-element.306), channel_id=1, source_target_pairs={{0,1},{1,2},{2,3},{4,5},{5,6},{6,7},{8,9},{9,10},{10,11},{12,13},{... | collective-permute-start | bytes 1160 | tf_op jit(solution)/shard_map/ppermute | solution.py:22
  69.2 0.7 copy-start.8
  69.3 0.7 copy-start.7
  70.0 7.9 %collective-permute-start.17 = (f32[1,32,128]{2,1,0:T(8,128)S(1)}, f32[1,32,128]{2,1,0:T(8,128)S(1)}, u32[]{:S(2)}, u32[]{:S(2)}) collective-permute-start(f32[1,32,128]{2,1,0:T(8,128)S(1)} %add_bitcast_fusion), channel_id=1, source_target_pairs={{4,0},{8,4},{12,8},{16,12},{20,16},{24,20},{28,24},{5,1},{9,5},{13... | collective-permute-start | bytes 49160 | tf_op jit(solution)/shard_map/ppermute | solution.py:25
  71.9 6.8 %collective-permute-start.16 = (f32[1,32,128]{2,1,0:T(8,128)S(1)}, f32[1,32,128]{2,1,0:T(8,128)S(1)}, u32[]{:S(2)}, u32[]{:S(2)}) collective-permute-start(f32[1,32,128]{2,1,0:T(8,128)S(1)} %add_bitcast_fusion), channel_id=1, source_target_pairs={{0,4},{4,8},{8,12},{12,16},{16,20},{20,24},{24,28},{1,5},{5,9},{9,... | collective-permute-start | bytes 49160 | tf_op jit(solution)/shard_map/ppermute | solution.py:22
  99.9 3.5 %copy-start.6 = (f32[32,128]{1,0:T(8,128)S(1)}, f32[32,128]{1,0:T(8,128)}, u32[]{:S(2)}) copy-start(f32[32,128]{1,0:T(8,128)} %param.15) | copy-start | bytes 49156
  99.9 3.5 %copy-start.10 = (s32[32]{0:T(128)S(1)}, s32[32]{0:T(128)}, u32[]{:S(2)}) copy-start(s32[32]{0:T(128)} %param.17) | copy-start | bytes 388
  113.3 57.9 %reduce-scatter.2.cloned.1.call-start = ((), (), s32[]{:S(2)}) async-start(), calls=%async_computation.2 | async-start | bytes 245760 | tf_op jit(solution)/shard_map/reduce_scatter | solution.py:175
  113.5 36.8 %copy-start.1 = (f32[384,128]{1,0:T(8,128)S(1)}, f32[384,128]{1,0:T(8,128)}, u32[]{:S(2)}) copy-start(f32[384,128]{1,0:T(8,128)} %copy-done) | copy-start | bytes 589828
  152.7 27.7 %collective-permute-start.19 = (f32[32,128]{1,0:T(8,128)S(1)}, f32[32,128]{1,0:T(8,128)S(1)}, u32[]{:S(2)}, u32[]{:S(2)}) collective-permute-start(f32[32,128]{1,0:T(8,128)S(1)} %get-tuple-element.301), channel_id=1, source_target_pairs={{0,4},{4,8},{8,12},{12,16},{16,20},{20,24},{24,28},{1,5},{5,9},{9,... | collective-permute-start | bytes 49160 | tf_op jit(solution)/shard_map/ppermute | solution.py:33
  158.2 22.2 %collective-permute-start.18 = (f32[32,128]{1,0:T(8,128)S(1)}, f32[32,128]{1,0:T(8,128)S(1)}, u32[]{:S(2)}, u32[]{:S(2)}) collective-permute-start(f32[32,128]{1,0:T(8,128)S(1)} %get-tuple-element.300), channel_id=1, source_target_pairs={{4,0},{8,4},{12,8},{16,12},{20,16},{24,20},{28,24},{5,1},{9,5},{13... | collective-permute-start | bytes 49160 | tf_op jit(solution)/shard_map/ppermute | solution.py:33
  172.0 8.4 %collective-permute-start.21 = (f32[32,128]{1,0:T(8,128)S(1)}, f32[32,128]{1,0:T(8,128)S(1)}, u32[]{:S(2)}, u32[]{:S(2)}) collective-permute-start(f32[32,128]{1,0:T(8,128)S(1)} %get-tuple-element.303), channel_id=1, source_target_pairs={{0,4},{4,8},{8,12},{12,16},{16,20},{20,24},{24,28},{1,5},{5,9},{9,... | collective-permute-start | bytes 49160 | tf_op jit(solution)/shard_map/ppermute | solution.py:33
  177.8 6.0 %collective-permute-start.20 = (f32[32,128]{1,0:T(8,128)S(1)}, f32[32,128]{1,0:T(8,128)S(1)}, u32[]{:S(2)}, u32[]{:S(2)}) collective-permute-start(f32[32,128]{1,0:T(8,128)S(1)} %get-tuple-element.302), channel_id=1, source_target_pairs={{4,0},{8,4},{12,8},{16,12},{20,16},{24,20},{28,24},{5,1},{9,5},{13... | collective-permute-start | bytes 49160 | tf_op jit(solution)/shard_map/ppermute | solution.py:33
  (3 other events, 2.1 us)
Sparse Core Ops, SparseCore 0:
  113.5 36.7 all-reduce.1
  152.5 18.6 reduce-scatter.1
where the time goes:
time: 193 us; the launch traced here: 192 us
  starting transfers between devices  76.3 us (40%)
  waiting for transfers between devices  54.5 us (28%)
  other arithmetic  21.9 us (11%)
  between operations  14.7 us (8%)
  blocking collectives  12.5 us (6%)
  local copies, waits for them, and re-layouts  9.33 us (5%)
  matrix products  2.29 us (1%)
    ppermute x9, starting transfers between devices, with_halo(): lax.ppermute(lax.slice_in_dim(block, block.shape[dim] - width, None, axis...  43.8 us
    pmax x1, waiting for transfers between devices, per_device(): top_three = lax.pmax(peak_three, 'tile')  33.2 us
    ppermute x9, starting transfers between devices, with_halo(): lax.ppermute(lax.slice_in_dim(block, 0, width, axis=dim), axis, backward)  17.2 us
    ppermute x4, starting transfers between devices, passed_along(): lax.ppermute(value, axis, [(source, source + steps) for source in range(l...  15.1 us
    all_gather x1, blocking collectives, per_device(): lax.all_gather(rimmed, 'tile', axis=1, tiled=True)  12.5 us
    reduce_scatter x1, waiting for transfers between devices, per_device(): lax.psum_scatter(scaled, 'tile', scatter_dimension=1, tiled=True)  11.1 us
    ppermute x9, waiting for transfers between devices, with_halo(): lax.ppermute(lax.slice_in_dim(block, block.shape[dim] - width, None, axis...  6.71 us
  transfers between devices with their start and end apart: 24, of which 12 were waited for; matrix products, arithmetic and copies ran while one was open for 3% of the time, Pallas kernels for 0%

commit v1 on v0

v1 whole, which is shorter than its diff:
```python
import functools
import math

import jax
import jax.numpy as jnp
from jax import lax
from jax.experimental import pallas as pl
from jax.experimental.pallas import tpu as pltpu
from jax.sharding import PartitionSpec as P

COARSE_ITERS = 2
REACH = 4
entropy = 0.5
damping = 0.8
coarse_power = 0.8
taps = [math.exp(-0.125 * k * k) for k in range(-REACH, REACH + 1)]
MESH = pl.DeviceIdType.MESH
NT = (((1,), (1,)), ((), ()))
NN = (((1,), (0,)), ((), ()))


def halves(x):
    high = x.astype(jnp.bfloat16)
    low = (x - high.astype(jnp.float32)).astype(jnp.bfloat16)
    return high, low


def dot(a, b):
    a_high, a_low = halves(a)
    b_high, b_low = halves(b)
    one = functools.partial(
        lax.dot_general, dimension_numbers=NN, preferred_element_type=jnp.float32
    )
    return one(a_high, b_high) + (one(a_high, b_low) + one(a_low, b_high))


def column_to_row(col, tiles):
    out = []
    for at in range(0, tiles, 128):
        eye = lax.broadcasted_iota(jnp.int32, (128, 128), 0) == lax.broadcasted_iota(
            jnp.int32, (128, 128), 1
        )
        part = jnp.where(eye, col[at : at + 128], 0.0)
        out.append(jnp.sum(part, axis=0, keepdims=True))
    return jnp.concatenate(out, axis=1)


def kernel(
    n_band,
    n_tile,
    cs_ref,
    ct_ref,
    off_ref,
    sm_ref,
    tm_ref,
    cnt_ref,
    pair_ref,
    u_ref,
    v_ref,
    sp_ref,
    tp_ref,
    coarse,
    ext,
    pairs,
    win1,
    win2,
    count1,
    count2,
    mix,
    c_send,
    c_recv,
    p_send,
    p_recv,
    w1_send,
    w1_recv,
    w2_send,
    w2_recv,
):
    rows, cols = cs_ref.shape
    tiles, width = off_ref.shape
    prow = pair_ref.shape[0] // 2
    band = lax.axis_index("band")
    tile = lax.axis_index("tile")
    f32 = jnp.float32
    keep = rows

    barrier = pltpu.get_barrier_semaphore()
    has_band = {-1: band > 0, 0: True, 1: band < n_band - 1}

    def when(cond, body):
        if cond is True:
            body()
        else:
            pl.when(cond)(body)

    partners = [
        (db, k) for db in (-1, 0, 1) for k in range(n_tile) if (db, k) != (0, 0)
    ]

    def device(db, k):
        return (band + db, lax.rem(tile + k, n_tile))

    for db, k in partners:

        def greet(db=db, k=k):
            pl.semaphore_signal(barrier, inc=1, device_id=device(db, k), device_id_type=MESH)

        when(has_band[db], greet)

    coarse[1, 1, 0:rows] = cs_ref[...]
    coarse[1, 1, rows : 2 * rows] = ct_ref[...]
    pairs[1, tile] = pair_ref[...]
    for db in (-1, 1):

        def blank(db=db):
            for dt in (-1, 0, 1):
                coarse[1 + db, 1 + dt] = jnp.zeros((2 * rows, cols), f32)
            for t in range(n_tile):
                pairs[1 + db, t] = jnp.full(pair_ref.shape, -1, jnp.int32)
                win1[1 + db, t] = jnp.zeros((tiles, width), f32)
                win2[1 + db, t] = jnp.zeros((tiles, width), f32)

        pl.when(jnp.logical_not(has_band[db]))(blank)
    for dt in (-1, 1):
        here = tile + dt

        @pl.when(jnp.logical_or(here < 0, here > n_tile - 1))
        def _(dt=dt):
            for db in (-1, 0, 1):
                coarse[1 + db, 1 + dt] = jnp.zeros((2 * rows, cols), f32)

    one_side = n_tile
    greeters = n_tile - 1
    greeters = greeters + jnp.where(band > 0, one_side, 0) + jnp.where(
        band < n_band - 1, one_side, 0
    )
    pl.semaphore_wait(barrier, greeters)

    def coarse_copy(db, dt):
        return pltpu.make_async_remote_copy(
            src_ref=coarse.at[1, 1],
            dst_ref=coarse.at[1 - db, 1 - dt],
            send_sem=c_send.at[1 + db, 1 + dt],
            recv_sem=c_recv.at[1 - db, 1 - dt],
            device_id=(band + db, tile + dt),
            device_id_type=MESH,
        )

    def coarse_in(db, dt):
        return pltpu.make_async_remote_copy(
            src_ref=coarse.at[1, 1],
            dst_ref=coarse.at[1 + db, 1 + dt],
            send_sem=c_send.at[1 - db, 1 - dt],
            recv_sem=c_recv.at[1 + db, 1 + dt],
            device_id=(band + db, tile + dt),
            device_id_type=MESH,
        )

    around = [(db, dt) for dt in (-1, 1, 0) for db in (-1, 0, 1) if (db, dt) != (0, 0)]

    def there(db, dt):
        ok = None
        for d, at, n in ((db, band, n_band), (dt, tile, n_tile)):
            if d:
                c = at > 0 if d < 0 else at < n - 1
                ok = c if ok is None else jnp.logical_and(ok, c)
        return ok

    for db, dt in around:
        when(there(db, dt), lambda db=db, dt=dt: coarse_copy(db, dt).start())

    def pair_copy(db, k):
        return pltpu.make_async_remote_copy(
            src_ref=pairs.at[1, tile],
            dst_ref=pairs.at[1 - db, tile],
            send_sem=p_send.at[1 + db, k],
            recv_sem=p_recv.at[1 - db, tile],
            device_id=device(db, k),
            device_id_type=MESH,
        )

    def pair_in(db, k):
        src = lax.rem(tile + k, n_tile)
        return pltpu.make_async_remote_copy(
            src_ref=pairs.at[1, tile],
            dst_ref=pairs.at[1 + db, src],
            send_sem=p_send.at[1 + db, k],
            recv_sem=p_recv.at[1 + db, src],
            device_id=device(db, k),
            device_id_type=MESH,
        )

    for db, k in partners:
        when(has_band[db], lambda db=db, k=k: pair_copy(db, k).start())

    full = n_tile * width
    scale = float(full * full) / 4.0 * entropy
    near_i = lax.broadcasted_iota(jnp.int32, (width, width), 0)
    near_j = lax.broadcasted_iota(jnp.int32, (width, width), 1)
    for t in range(n_tile):
        gap = ((t - tile) * width + near_i - near_j).astype(f32)
        mix[t] = jnp.exp(gap * gap * (-1.0 / scale))

    lanes = pair_ref.shape[1]
    base = (band - 1) * n_tile * tiles
    window = 3 * n_tile * tiles
    total = jnp.zeros((tiles, window), f32)
    for r in range(prow):
        src = pair_ref[r : r + 1, :]
        tgt = pair_ref[prow + r : prow + r + 1, :] - base
        a = jnp.where(
            lax.broadcasted_iota(jnp.int32, (tiles, lanes), 0) == src, 1.0, 0.0
        ).astype(jnp.bfloat16)
        b = jnp.where(
            lax.broadcasted_iota(jnp.int32, (window, lanes), 0) == tgt, 1.0, 0.0
        ).astype(jnp.bfloat16)
        total = total + lax.dot_general(a, b, NT, preferred_element_type=f32)
    lane = lax.broadcasted_iota(jnp.int32, (tiles, window), 1)
    own = lax.broadcasted_iota(jnp.int32, (tiles, window), 0)
    drow = (
        own + tiles - (lane // (n_tile * tiles)) * tiles - lane % tiles
    ).astype(f32)
    damp = drow * drow * (-1.0 / scale)
    count1[...] = total

    for db, dt in around:
        when(there(db, dt), lambda db=db, dt=dt: coarse_in(db, dt).wait_recv())

    span_r = rows + 2 * keep
    wide = 2 * cols
    grid_rows = n_band * rows
    for which in range(2):
        for db in (-1, 0, 1):
            lo = which * rows
            if db == -1:
                rs, rd = slice(lo + rows - keep, lo + rows), slice(0, keep)
            elif db == 0:
                rs, rd = slice(lo, lo + rows), slice(keep, keep + rows)
            else:
                rs, rd = slice(lo, lo + keep), slice(keep + rows, span_r)
            ext[which, rd, 0:cols] = coarse[1 + db, 1, rs]
            lane2 = lax.broadcasted_iota(jnp.int32, (keep if db else rows, cols), 1)
            ext[which, rd, cols:wide] = jnp.where(
                lane2 < cols // 2, coarse[1 + db, 2, rs], coarse[1 + db, 0, rs]
            )
    src_ext = ext[0]
    tgt_ext = ext[1]
    row_at = lax.broadcasted_iota(jnp.int32, (span_r, wide), 0) + band * rows - keep
    lane_at = lax.broadcasted_iota(jnp.int32, (span_r, wide), 1)
    col_at = jnp.where(lane_at < cols + cols // 2, lane_at, lane_at - wide) + tile * cols
    inside = jnp.logical_and(
        jnp.logical_and(row_at >= 0, row_at < grid_rows),
        jnp.logical_and(col_at >= 0, col_at < n_tile * cols),
    )

    def blur(field, lost):
        n = field.shape[0] - 2 * REACH
        across = taps[0] * field[0:n]
        for k in range(1, 2 * REACH + 1):
            across = across + taps[k] * field[k : k + n]
        result = taps[REACH] * across
        for k in range(1, REACH + 1):
            result = result + taps[REACH + k] * (
                pltpu.roll(across, k, 1) + pltpu.roll(across, wide - k, 1)
            )
        return result

    def power(x):
        return jnp.exp(coarse_power * jnp.log(x))

    def ones_blur(position, count):
        out = jnp.zeros(position.shape, f32)
        for k in range(-REACH, REACH + 1):
            at = position + k
            out = out + jnp.where(jnp.logical_and(at >= 0, at < count), taps[REACH + k], 0.0)
        return out

    edge_r = ones_blur(row_at[:, 0:1], grid_rows)
    edge_c = ones_blur(col_at[0:1, :], n_tile * cols)
    spread = edge_r * edge_c
    safe = jnp.where(inside, spread, 1.0)
    safe_src = jnp.where(inside, src_ext, 1.0)
    safe_tgt = jnp.where(inside, tgt_ext, 1.0)
    u = jnp.where(inside, power(safe_src / safe), 0.0)
    for lost in (4, 8, 12):
        field = u if lost == 4 else (v if lost == 8 else u)
        out = blur(field, lost)
        s = slice(lost, span_r - lost)
        mask = inside[s]
        mass = safe_src[s] if lost == 8 else safe_tgt[s]
        res = jnp.where(mask, power(mass / jnp.where(mask, out, 1.0)), 0.0)
        if lost == 8:
            u = res
        else:
            v = res
    u_ref[...] = u[keep - 8 : keep - 8 + rows, 0:cols]
    scaling_v = v[keep - 12 : keep - 12 + rows, 0:cols]
    v_ref[...] = scaling_v

    fold = tiles // rows
    log_v = jnp.log(scaling_v)
    parent = jnp.broadcast_to(log_v[:, None, :], (rows, fold, cols)).reshape(tiles, cols)
    field = (off_ref[...] + entropy * parent) / entropy + jnp.log(tm_ref[...])

    def gather(win, send, recv, value, between):
        win[1, tile] = value

        def over_tile(k):
            return pltpu.make_async_remote_copy(
                src_ref=win.at[1, tile],
                dst_ref=win.at[1, tile],
                send_sem=send.at[1, k],
                recv_sem=recv.at[1, tile],
                device_id=device(0, k),
                device_id_type=MESH,
            )

        def over_band(db, k):
            src = lax.rem(tile + k, n_tile)
            return pltpu.make_async_remote_copy(
                src_ref=win.at[1, src],
                dst_ref=win.at[1 - db, src],
                send_sem=send.at[1 + db, k],
                recv_sem=recv.at[1 - db, src],
                device_id=device(db, 0),
                device_id_type=MESH,
            )

        def arrive(db, k):
            src = lax.rem(tile + k, n_tile)
            return pltpu.make_async_remote_copy(
                src_ref=win.at[1, src],
                dst_ref=win.at[1 + db, src],
                send_sem=send.at[1 + db, k],
                recv_sem=recv.at[1 + db, src],
                device_id=device(db, 0) if db else device(0, k),
                device_id_type=MESH,
            )

        order = sorted(range(1, n_tile), key=lambda k: min(k, n_tile - k))
        for k in reversed(order):
            over_tile(k).start()
        for db in (-1, 1):
            when(has_band[db], lambda db=db: over_band(db, 0).start())
        between()
        for k in order:
            arrive(0, k).wait_recv()
            for db in (-1, 1):
                when(has_band[db], lambda db=db, k=k: over_band(db, k).start())
        for db in (-1, 1):

            def take(db=db):
                for k in [0] + order:
                    arrive(db, k).wait_recv()

            when(has_band[db], take)

        def finish():
            for k in order:
                over_tile(k).wait_send()
            for db in (-1, 1):

                def sent(db=db):
                    for k in range(n_tile):
                        over_band(db, k).wait_send()

                when(has_band[db], sent)

        return finish

    def reduce(win, count):
        values = win[...]
        flat = values.reshape(window, width)
        high = jnp.max(flat, axis=1, keepdims=True)
        near = jnp.exp(flat - high)
        blocks = near.reshape(3, n_tile, tiles, width)
        parts = [
            dot(blocks[:, t].reshape(3 * tiles, width), mix[t]).reshape(3, 1, tiles, width)
            for t in range(n_tile)
        ]
        spread = jnp.concatenate(parts, axis=1).reshape(window, width)
        high_row = column_to_row(high, window)
        n = count[...]
        lifted = jnp.where(n > 0.0, high_row + damp, -jnp.inf)
        peak = jnp.max(lifted, axis=1, keepdims=True)
        peak = jnp.where(peak == -jnp.inf, 0.0, peak)
        weight = n * jnp.exp(lifted - peak)
        summed = dot(weight, spread)
        return peak + jnp.log(summed)

    def incoming_counts():
        for db, k in partners:
            when(has_band[db], lambda db=db, k=k: pair_in(db, k).wait_recv())
        mine = (band * n_tile + tile) * tiles
        parts = []
        for b in range(3):
            for t in range(n_tile):
                here = pairs[b, t]
                part = jnp.zeros((tiles, tiles), f32)
                for r in range(prow):
                    src = here[r : r + 1]
                    tgt = here[prow + r : prow + r + 1] - mine
                    live = lax.broadcasted_iota(jnp.int32, (tiles, lanes), 0)
                    a = jnp.where(live == src, 1.0, 0.0).astype(jnp.bfloat16)
                    c = jnp.where(live == tgt, 1.0, 0.0).astype(jnp.bfloat16)
                    part = part + lax.dot_general(c, a, NT, preferred_element_type=f32)
                parts.append(part)
        count2[...] = jnp.concatenate(parts, axis=1)

    finish1 = gather(win1, w1_send, w1_recv, field, incoming_counts)
    potential = -damping * entropy * reduce(win1, count1)
    sp_ref[...] = potential
    eye = lax.broadcasted_iota(jnp.int32, (tiles, tiles), 0) == lax.broadcasted_iota(
        jnp.int32, (tiles, tiles), 1
    )
    cell_count = jnp.sum(jnp.where(eye, cnt_ref[...].astype(f32), 0.0), axis=1, keepdims=True)
    active = lax.broadcasted_iota(jnp.int32, (tiles, width), 1).astype(f32) < cell_count
    source_field = jnp.where(active, potential / entropy + jnp.log(sm_ref[...]), -jnp.inf)
    finish2 = gather(win2, w2_send, w2_recv, source_field, lambda: None)
    tp_ref[...] = -damping * entropy * reduce(win2, count2)

    for db, dt in around:
        when(there(db, dt), lambda db=db, dt=dt: coarse_copy(db, dt).wait_send())
    for db, k in partners:
        when(has_band[db], lambda db=db, k=k: pair_copy(db, k).wait_send())
    finish1()
    finish2()


def per_device(cs, ct, off, sm, tm, cnt, ps, pt):
    n_band = lax.axis_size("band")
    n_tile = lax.axis_size("tile")
    rows, cols = cs.shape
    tiles, width = off.shape
    pair = jnp.concatenate([ps.reshape(-1, 128), pt.reshape(-1, 128)], axis=0)
    f32 = jnp.float32
    window = 3 * n_tile * tiles
    dma = pltpu.SemaphoreType.DMA
    return pl.pallas_call(
        functools.partial(kernel, n_band, n_tile),
        out_shape=(
            jax.ShapeDtypeStruct((rows, cols), f32),
            jax.ShapeDtypeStruct((rows, cols), f32),
            jax.ShapeDtypeStruct((tiles, width), f32),
            jax.ShapeDtypeStruct((tiles, width), f32),
        ),
        in_specs=[pl.BlockSpec(memory_space=pltpu.VMEM)] * 7,
        out_specs=[pl.BlockSpec(memory_space=pltpu.VMEM)] * 4,
        scratch_shapes=[
            pltpu.VMEM((3, 3, 2 * rows, cols), f32),
            pltpu.VMEM((2, 3 * rows, 2 * cols), f32),
            pltpu.VMEM((3, n_tile) + pair.shape, jnp.int32),
            pltpu.VMEM((3, n_tile, tiles, width), f32),
            pltpu.VMEM((3, n_tile, tiles, width), f32),
            pltpu.VMEM((tiles, window), f32),
            pltpu.VMEM((tiles, window), f32),
            pltpu.VMEM((n_tile, width, width), f32),
            dma((3, 3)),
            dma((3, 3)),
            dma((3, n_tile)),
            dma((3, n_tile)),
            dma((3, n_tile)),
            dma((3, n_tile)),
            dma((3, n_tile)),
            dma((3, n_tile)),
        ],
        compiler_params=pltpu.CompilerParams(
            collective_id=0, has_side_effects=True, vmem_limit_bytes=32 * 1024 * 1024
        ),
    )(cs, ct, off, sm, tm, cnt.reshape(1, tiles), pair)


def solution(mesh):
    placed = (
        P("band", "tile"),
        P("band", "tile"),
        P(("band", "tile"), None),
        P(("band", "tile"), None),
        P(("band", "tile"), None),
        P(("band", "tile")),
        P(("band", "tile")),
        P(("band", "tile")),
    )
    return jax.shard_map(
        per_device,
        mesh=mesh,
        in_specs=placed,
        out_specs=(
            P("band", "tile"),
            P("band", "tile"),
            P(("band", "tile"), None),
            P(("band", "tile"), None),
        ),
        check_vma=False,
    )
```

time: 193 us -> 31.3 us (0.16)
  starting transfers between devices: 76.3 us -> 0 us
  waiting for transfers between devices: 54.5 us -> 0 us
  Pallas kernels: 0 us -> 24.1 us
  other arithmetic: 21.9 us -> 0.72 us
  between operations: 14.7 us -> 0.67 us
  blocking collectives: 12.5 us -> 0 us
  local copies, waits for them, and re-layouts: 9.33 us -> 5.26 us
  matrix products: 2.29 us -> 0 us
    ppermute x22 -> x0, starting transfers between devices: 76.2 us -> none  [the longest x9 43.8 us: with_halo(): lax.ppermute(lax.slice_in_dim(block, block.shape[dim] - width, None, axis...]
    pmax x1 -> x0, waiting for transfers between devices: 33.2 us -> none  [per_device(): top_three = lax.pmax(peak_three, 'tile')]
    pallas_call x0 -> x1, Pallas kernels: none -> 24.1 us  [per_device(): pl.pallas_call(functools.partial(kernel, n_band, n_tile), out_shape=(jax....]
    all_gather x1 -> x0, blocking collectives: 12.5 us -> none  [per_device(): lax.all_gather(rimmed, 'tile', axis=1, tiled=True)]
    reduce_scatter x1 -> x0, waiting for transfers between devices: 11.1 us -> none  [per_device(): lax.psum_scatter(scaled, 'tile', scatter_dimension=1, tiled=True)]
    ppermute x22 -> x0, waiting for transfers between devices: 10.1 us -> none  [the longest x9 6.71 us: with_halo(): lax.ppermute(lax.slice_in_dim(block, block.shape[dim] - width, None, axis...]
    another operation x2 -> x0, other arithmetic: 7.07 us -> none  [the longest x1 3.57 us: per_device(): win_peak = jnp.full((window_tiles, width), neg, jnp.float32).at[where_win...]
    scatter-add x2 -> x0, other arithmetic: 7.07 us -> none  [the longest x1 3.57 us: per_device(): jnp.zeros((window_tiles, width), jnp.float32).at[where_window].add(weighted)]
  transfers between devices with their start and end apart: 24 -> 0, of which waited for: 12 -> 0; matrix products, arithmetic and copies ran while one was open for 3% -> 0% of each run, Pallas kernels for 0% -> 0%
where the time goes in v1:
time: 31.3 us; the launch traced here: 30.7 us
  Pallas kernels  24.1 us (77%)
  local copies, waits for them, and re-layouts  5.26 us (17%)
  other arithmetic  0.72 us (2%)
  between operations  0.67 us (2%)
    pallas_call x1, Pallas kernels, per_device(): pl.pallas_call(functools.partial(kernel, n_band, n_tile), out_shape=(jax....  24.1 us
    unnamed x16, local copies, waits for them, and re-layouts  5.26 us
    concatenate x1, other arithmetic, per_device(): pair = jnp.concatenate([ps.reshape(-1, 128), pt.reshape(-1, 128)], axis=0)  0.72 us

profile of v1, /device:TPU:3, one launch (start us, length us, event | category | flops | bytes accessed | tf_op | source)
XLA Modules:
  0.0 30.7 jit_solution(4911803245037164480)
XLA Ops:
  0.6 0.0 copy-start.3
  0.6 0.0 copy-start.5
  0.7 0.7 %pad_add_fusion.pair_ref = s32[8,128]{1,0:T(8,128)S(1)} fusion(s32[4,128]{1,0:T(4,128)} %bitcast.4, s32[4,128]{1,0:T(4,128)} %bitcast.5), kind=kLoop, calls=%fused_computation | loop fusion | flops 1024 | bytes 8192 | tf_op jit(solution)/shard_map/concatenate | solution.py:435
  1.4 0.0 copy-done.3
  1.4 0.0 copy-done.5
  1.4 0.0 copy-start
  1.4 0.7 %copy-done = f32[32,128]{1,0:T(8,128)S(1)} copy-done((f32[32,128]{1,0:T(8,128)S(1)}, f32[32,128]{1,0:T(8,128)}, u32[]{:S(2)}) %copy-start) | copy-done | bytes 16408
  2.1 0.0 copy-start.1
  2.1 0.7 %copy-done.1 = f32[32,128]{1,0:T(8,128)S(1)} copy-done((f32[32,128]{1,0:T(8,128)S(1)}, f32[32,128]{1,0:T(8,128)}, u32[]{:S(2)}) %copy-start.1) | copy-done | bytes 16408
  2.8 0.0 copy-start.2
  2.8 0.7 %copy-done.2 = f32[32,128]{1,0:T(8,128)S(1)} copy-done((f32[32,128]{1,0:T(8,128)S(1)}, f32[32,128]{1,0:T(8,128)}, u32[]{:S(2)}) %copy-start.2) | copy-done | bytes 16408
  3.5 0.0 copy-start.4
  3.5 0.7 %copy-done.4 = f32[16,128]{1,0:T(8,128)S(1)} copy-done((f32[16,128]{1,0:T(8,128)S(1)}, f32[16,128]{1,0:T(8,128)}, u32[]{:S(2)}) %copy-start.4) | copy-done | bytes 8216
  4.2 24.1 %shard_map.111 = (f32[16,128]{1,0:T(8,128)S(1)}, f32[16,128]{1,0:T(8,128)S(1)}, f32[32,128]{1,0:T(8,128)S(1)}, f32[32,128]{1,0:T(8,128)S(1)}) custom-call(f32[16,128]{1,0:T(8,128)S(1)} %copy-done.3, f32[16,128]{1,0:T(8,128)S(1)} %copy-done.4, f32[32,128]{1,0:T(8,128)S(1)} %copy-done, f32[32,128]{1,0:T(8,128)S(1)} %copy-done.1, f32[32,128]{1,0:T(8,128)S(1)} %copy-done.2, ...), custom_call_target="tpu_custom_call" | custom-call | tf_op jit(solution)/shard_map/pallas_call | solution.py:439
  28.3 0.6 %copy.16 = f32[16,128]{1,0:T(8,128)} copy(f32[16,128]{1,0:T(8,128)S(1)} %get-tuple-element.8) | data formatting | bytes 16384
  28.9 0.6 %copy.17 = f32[16,128]{1,0:T(8,128)} copy(f32[16,128]{1,0:T(8,128)S(1)} %get-tuple-element.9) | data formatting | bytes 16384
  29.5 0.6 %copy.18 = f32[32,128]{1,0:T(8,128)} copy(f32[32,128]{1,0:T(8,128)S(1)} %get-tuple-element.10) | data formatting | bytes 32768
  30.1 0.6 %copy.19 = f32[32,128]{1,0:T(8,128)} copy(f32[32,128]{1,0:T(8,128)S(1)} %get-tuple-element.11) | data formatting | bytes 32768
Async XLA Ops:
  0.6 0.7 %copy-start.3 = (f32[16,128]{1,0:T(8,128)S(1)}, f32[16,128]{1,0:T(8,128)}, u32[]{:S(2)}) copy-start(f32[16,128]{1,0:T(8,128)} %cs_ref.1) | copy-start | bytes 24580
  0.6 0.7 %copy-start.5 = (s32[32]{0:T(128)S(1)}, s32[32]{0:T(128)}, u32[]{:S(2)}) copy-start(s32[32]{0:T(128)} %param.13) | copy-start | bytes 388
  1.4 0.7 %copy-start = (f32[32,128]{1,0:T(8,128)S(1)}, f32[32,128]{1,0:T(8,128)}, u32[]{:S(2)}) copy-start(f32[32,128]{1,0:T(8,128)} %off_ref.1) | copy-start | bytes 49156
  2.1 0.7 %copy-start.1 = (f32[32,128]{1,0:T(8,128)S(1)}, f32[32,128]{1,0:T(8,128)}, u32[]{:S(2)}) copy-start(f32[32,128]{1,0:T(8,128)} %sm_ref.1) | copy-start | bytes 49156
  2.8 0.7 %copy-start.2 = (f32[32,128]{1,0:T(8,128)S(1)}, f32[32,128]{1,0:T(8,128)}, u32[]{:S(2)}) copy-start(f32[32,128]{1,0:T(8,128)} %tm_ref.1) | copy-start | bytes 49156
  3.5 0.7 %copy-start.4 = (f32[16,128]{1,0:T(8,128)S(1)}, f32[16,128]{1,0:T(8,128)}, u32[]{:S(2)}) copy-start(f32[16,128]{1,0:T(8,128)} %ct_ref.1) | copy-start | bytes 24580

commit v2 on v1

--- a/solution.py
+++ b/solution.py
@@ -25,15 +25,6 @@
     return high, low
 
 
-def dot(a, b):
-    a_high, a_low = halves(a)
-    b_high, b_low = halves(b)
-    one = functools.partial(
-        lax.dot_general, dimension_numbers=NN, preferred_element_type=jnp.float32
-    )
-    return one(a_high, b_high) + (one(a_high, b_low) + one(a_low, b_high))
-
-
 def column_to_row(col, tiles):
     out = []
     for at in range(0, tiles, 128):
@@ -54,12 +45,23 @@
     sm_ref,
     tm_ref,
     cnt_ref,
-    pair_ref,
+    ps_ref,
+    pt_ref,
     u_ref,
     v_ref,
     sp_ref,
     tp_ref,
+    fine,
+    cells,
+    arrived,
+    u_out,
+    v_out,
+    sp_out,
+    tp_out,
+    stored,
     coarse,
+    side,
+    edges,
     ext,
     pairs,
     win1,
@@ -67,6 +69,8 @@
     count1,
     count2,
     mix,
+    spread,
+    peaks,
     c_send,
     c_recv,
     p_send,
@@ -78,7 +82,7 @@
 ):
     rows, cols = cs_ref.shape
     tiles, width = off_ref.shape
-    prow = pair_ref.shape[0] // 2
+    slots = ps_ref.shape[1]
     band = lax.axis_index("band")
     tile = lax.axis_index("tile")
     f32 = jnp.float32
@@ -107,18 +111,39 @@
 
         when(has_band[db], greet)
 
-    coarse[1, 1, 0:rows] = cs_ref[...]
-    coarse[1, 1, rows : 2 * rows] = ct_ref[...]
-    pairs[1, tile] = pair_ref[...]
+    loads = [
+        pltpu.make_async_copy(src, dst, arrived.at[i])
+        for i, (src, dst) in enumerate(
+            (
+                (cs_ref, coarse.at[1, 0]),
+                (ct_ref, coarse.at[1, 1]),
+                (ps_ref, pairs.at[1, tile, 0]),
+                (pt_ref, pairs.at[1, tile, 1]),
+                (off_ref, fine.at[0]),
+                (tm_ref, fine.at[1]),
+                (sm_ref, fine.at[2]),
+                (cnt_ref, cells),
+            )
+        )
+    ]
+    for load in loads:
+        load.start()
+    stores = [
+        pltpu.make_async_copy(src, dst, stored.at[i])
+        for i, (src, dst) in enumerate(
+            ((u_out, u_ref), (v_out, v_ref), (sp_out, sp_ref), (tp_out, tp_ref))
+        )
+    ]
     for db in (-1, 1):
 
         def blank(db=db):
-            for dt in (-1, 0, 1):
-                coarse[1 + db, 1 + dt] = jnp.zeros((2 * rows, cols), f32)
+            coarse[1 + db] = jnp.zeros((2, rows, cols), f32)
             for t in range(n_tile):
-                pairs[1 + db, t] = jnp.full(pair_ref.shape, -1, jnp.int32)
+                pairs[1 + db, t] = jnp.full((2, 1, slots), -1, jnp.int32)
                 win1[1 + db, t] = jnp.zeros((tiles, width), f32)
                 win2[1 + db, t] = jnp.zeros((tiles, width), f32)
+            for dt in range(2):
+                side[1 + db, dt] = jnp.zeros((rows, cols), f32)
 
         pl.when(jnp.logical_not(has_band[db]))(blank)
     for dt in (-1, 1):
@@ -127,8 +152,16 @@
         @pl.when(jnp.logical_or(here < 0, here > n_tile - 1))
         def _(dt=dt):
             for db in (-1, 0, 1):
-                coarse[1 + db, 1 + dt] = jnp.zeros((2 * rows, cols), f32)
-
+                side[1 + db, (1 + dt) // 2] = jnp.zeros((rows, cols), f32)
+
+    half = cols // 2
+    edge_lane = lax.broadcasted_iota(jnp.int32, (rows, cols), 1)
+    loads[0].wait()
+    loads[1].wait()
+    own_cs = coarse[1, 0]
+    turned = pltpu.roll(coarse[1, 1], half, 1)
+    edges[1] = jnp.where(edge_lane >= half, own_cs, turned)
+    edges[0] = jnp.where(edge_lane < half, own_cs, turned)
     one_side = n_tile
     greeters = n_tile - 1
     greeters = greeters + jnp.where(band > 0, one_side, 0) + jnp.where(
@@ -136,10 +169,15 @@
     )
     pl.semaphore_wait(barrier, greeters)
 
+    def coarse_refs(db, dt):
+        if dt == 0:
+            return coarse.at[1], coarse.at[1 + db]
+        return edges.at[(1 - dt) // 2], side.at[1 + db, (1 + dt) // 2]
+
     def coarse_copy(db, dt):
         return pltpu.make_async_remote_copy(
-            src_ref=coarse.at[1, 1],
-            dst_ref=coarse.at[1 - db, 1 - dt],
+            src_ref=coarse_refs(-db, -dt)[0],
+            dst_ref=coarse_refs(-db, -dt)[1],
             send_sem=c_send.at[1 + db, 1 + dt],
             recv_sem=c_recv.at[1 - db, 1 - dt],
             device_id=(band + db, tile + dt),
@@ -148,8 +186,8 @@
 
     def coarse_in(db, dt):
         return pltpu.make_async_remote_copy(
-            src_ref=coarse.at[1, 1],
-            dst_ref=coarse.at[1 + db, 1 + dt],
+            src_ref=coarse_refs(db, dt)[0],
+            dst_ref=coarse_refs(db, dt)[1],
             send_sem=c_send.at[1 - db, 1 - dt],
             recv_sem=c_recv.at[1 + db, 1 + dt],
             device_id=(band + db, tile + dt),
@@ -190,6 +228,8 @@
             device_id_type=MESH,
         )
 
+    loads[2].wait()
+    loads[3].wait()
     for db, k in partners:
         when(has_band[db], lambda db=db, k=k: pair_copy(db, k).start())
 
@@ -197,24 +237,33 @@
     scale = float(full * full) / 4.0 * entropy
     near_i = lax.broadcasted_iota(jnp.int32, (width, width), 0)
     near_j = lax.broadcasted_iota(jnp.int32, (width, width), 1)
+    mix_high, mix_low = halves(jnp.exp((near_i * near_j).astype(f32) * (2.0 / scale)))
+    mix[0:width, 0:width] = mix_high
+    mix[width : 2 * width, 0:width] = mix_high
+    mix[0:width, width : 2 * width] = mix_low
+    mix[width : 2 * width, width : 2 * width] = jnp.zeros((width, width), jnp.bfloat16)
+    cell = lax.broadcasted_iota(jnp.int32, (1, width), 1)
+    lift, ease = [], []
     for t in range(n_tile):
-        gap = ((t - tile) * width + near_i - near_j).astype(f32)
-        mix[t] = jnp.exp(gap * gap * (-1.0 / scale))
-
-    lanes = pair_ref.shape[1]
+        gap = (t - tile) * width
+        lift.append((-cell * cell - 2 * gap * cell).astype(f32) * (1.0 / scale))
+        rest = (gap - cell).astype(f32)
+        ease.append(jnp.exp(rest * rest * (-1.0 / scale)))
+
     base = (band - 1) * n_tile * tiles
     window = 3 * n_tile * tiles
-    total = jnp.zeros((tiles, window), f32)
-    for r in range(prow):
-        src = pair_ref[r : r + 1, :]
-        tgt = pair_ref[prow + r : prow + r + 1, :] - base
-        a = jnp.where(
-            lax.broadcasted_iota(jnp.int32, (tiles, lanes), 0) == src, 1.0, 0.0
+
+    def hits(count, index):
+        return jnp.where(
+            lax.broadcasted_iota(jnp.int32, (count, slots), 0) == index, 1.0, 0.0
         ).astype(jnp.bfloat16)
-        b = jnp.where(
-            lax.broadcasted_iota(jnp.int32, (window, lanes), 0) == tgt, 1.0, 0.0
-        ).astype(jnp.bfloat16)
-        total = total + lax.dot_general(a, b, NT, preferred_element_type=f32)
+
+    total = lax.dot_general(
+        hits(tiles, pairs[1, tile, 0]),
+        hits(window, pairs[1, tile, 1] - base),
+        NT,
+        preferred_element_type=f32,
+    )
     lane = lax.broadcasted_iota(jnp.int32, (tiles, window), 1)
     own = lax.broadcasted_iota(jnp.int32, (tiles, window), 0)
     drow = (
@@ -238,11 +287,14 @@
                 rs, rd = slice(lo, lo + rows), slice(keep, keep + rows)
             else:
                 rs, rd = slice(lo, lo + keep), slice(keep + rows, span_r)
-            ext[which, rd, 0:cols] = coarse[1 + db, 1, rs]
-            lane2 = lax.broadcasted_iota(jnp.int32, (keep if db else rows, cols), 1)
-            ext[which, rd, cols:wide] = jnp.where(
-                lane2 < cols // 2, coarse[1 + db, 2, rs], coarse[1 + db, 0, rs]
-            )
+            rs = slice(rs.start - lo, rs.stop - lo)
+            ext[which, rd, 0:cols] = coarse[1 + db, which, rs]
+            left, right = side[1 + db, 0, rs], side[1 + db, 1, rs]
+            if which == 0:
+                both = jnp.where(edge_lane < half, right, left)
+            else:
+                both = pltpu.roll(jnp.where(edge_lane < half, left, right), half, 1)
+            ext[which, rd, cols:wide] = both
     src_ext = ext[0]
     tgt_ext = ext[1]
     row_at = lax.broadcasted_iota(jnp.int32, (span_r, wide), 0) + band * rows - keep
@@ -277,8 +329,7 @@
 
     edge_r = ones_blur(row_at[:, 0:1], grid_rows)
     edge_c = ones_blur(col_at[0:1, :], n_tile * cols)
-    spread = edge_r * edge_c
-    safe = jnp.where(inside, spread, 1.0)
+    safe = jnp.where(inside, edge_r * edge_c, 1.0)
     safe_src = jnp.where(inside, src_ext, 1.0)
     safe_tgt = jnp.where(inside, tgt_ext, 1.0)
     u = jnp.where(inside, power(safe_src / safe), 0.0)
@@ -293,16 +344,20 @@
             u = res
         else:
             v = res
-    u_ref[...] = u[keep - 8 : keep - 8 + rows, 0:cols]
+    u_out[...] = u[keep - 8 : keep - 8 + rows, 0:cols]
     scaling_v = v[keep - 12 : keep - 12 + rows, 0:cols]
-    v_ref[...] = scaling_v
+    v_out[...] = scaling_v
+    stores[0].start()
+    stores[1].start()
 
     fold = tiles // rows
     log_v = jnp.log(scaling_v)
     parent = jnp.broadcast_to(log_v[:, None, :], (rows, fold, cols)).reshape(tiles, cols)
-    field = (off_ref[...] + entropy * parent) / entropy + jnp.log(tm_ref[...])
-
-    def gather(win, send, recv, value, between):
+    for load in loads[4:]:
+        load.wait()
+    field = (fine[0] + entropy * parent) / entropy + jnp.log(fine[1])
+
+    def gather(win, send, recv, value, between, absorb):
         win[1, tile] = value
 
         def over_tile(k):
@@ -347,6 +402,7 @@
             arrive(0, k).wait_recv()
             for db in (-1, 1):
                 when(has_band[db], lambda db=db, k=k: over_band(db, k).start())
+        absorb(1)
         for db in (-1, 1):
 
             def take(db=db):
@@ -354,6 +410,7 @@
                     arrive(db, k).wait_recv()
 
             when(has_band[db], take)
+            absorb(1 + db)
 
         def finish():
             for k in order:
@@ -368,56 +425,75 @@
 
         return finish
 
-    def reduce(win, count):
-        values = win[...]
-        flat = values.reshape(window, width)
-        high = jnp.max(flat, axis=1, keepdims=True)
-        near = jnp.exp(flat - high)
-        blocks = near.reshape(3, n_tile, tiles, width)
-        parts = [
-            dot(blocks[:, t].reshape(3 * tiles, width), mix[t]).reshape(3, 1, tiles, width)
-            for t in range(n_tile)
-        ]
-        spread = jnp.concatenate(parts, axis=1).reshape(window, width)
-        high_row = column_to_row(high, window)
+    per_band = n_tile * tiles
+
+    def absorber(win):
+        def absorb(b):
+            lifted = jnp.concatenate([win[b, t] + lift[t] for t in range(n_tile)], axis=0)
+            high = jnp.max(lifted, axis=1, keepdims=True)
+            near = jnp.concatenate(halves(jnp.exp(lifted - high)), axis=1)
+            out = lax.dot_general(near, mix[...], NN, preferred_element_type=f32)
+            out = out[:, 0:width] + out[:, width : 2 * width]
+            for t in range(n_tile):
+                part = out[t * tiles : (t + 1) * tiles] * ease[t]
+                part_high, part_low = halves(part)
+                rows_at = slice(b * per_band + t * tiles, b * per_band + (t + 1) * tiles)
+                spread[rows_at, 0:width] = part_high
+                spread[rows_at, width : 2 * width] = part_low
+            peaks[:, b * per_band : (b + 1) * per_band] = column_to_row(high, per_band)
+
+        return absorb
+
+    def reduce(count):
         n = count[...]
-        lifted = jnp.where(n > 0.0, high_row + damp, -jnp.inf)
+        lifted = jnp.where(n > 0.0, peaks[...] + damp, -jnp.inf)
         peak = jnp.max(lifted, axis=1, keepdims=True)
-        peak = jnp.where(peak == -jnp.inf, 0.0, peak)
         weight = n * jnp.exp(lifted - peak)
-        summed = dot(weight, spread)
+        both = jnp.concatenate(halves(weight), axis=0)
+        out = lax.dot_general(both, spread[...], NN, preferred_element_type=f32)
+        summed = out[0:tiles, 0:width] + (
+            out[tiles : 2 * tiles, 0:width] + out[0:tiles, width : 2 * width]
+        )
         return peak + jnp.log(summed)
 
-    def incoming_counts():
+    mine = (band * n_tile + tile) * tiles
+
+    def counts_of(b, t):
+        at = (b * n_tile + t) * tiles
+        count2[:, at : at + tiles] = lax.dot_general(
+            hits(tiles, pairs[b, t, 1] - mine),
+            hits(tiles, pairs[b, t, 0]),
+            NT,
+            preferred_element_type=f32,
+        )
+
+    blocks = [(b, t) for b in range(3) for t in range(n_tile)]
+
+    def early_counts():
         for db, k in partners:
             when(has_band[db], lambda db=db, k=k: pair_in(db, k).wait_recv())
-        mine = (band * n_tile + tile) * tiles
-        parts = []
-        for b in range(3):
-            for t in range(n_tile):
-                here = pairs[b, t]
-                part = jnp.zeros((tiles, tiles), f32)
-                for r in range(prow):
-                    src = here[r : r + 1]
-                    tgt = here[prow + r : prow + r + 1] - mine
-                    live = lax.broadcasted_iota(jnp.int32, (tiles, lanes), 0)
-                    a = jnp.where(live == src, 1.0, 0.0).astype(jnp.bfloat16)
-                    c = jnp.where(live == tgt, 1.0, 0.0).astype(jnp.bfloat16)
-                    part = part + lax.dot_general(c, a, NT, preferred_element_type=f32)
-                parts.append(part)
-        count2[...] = jnp.concatenate(parts, axis=1)
-
-    finish1 = gather(win1, w1_send, w1_recv, field, incoming_counts)
-    potential = -damping * entropy * reduce(win1, count1)
-    sp_ref[...] = potential
+        for b, t in blocks[0 : len(blocks) // 2]:
+            counts_of(b, t)
+
+    def late_counts():
+        for b, t in blocks[len(blocks) // 2 :]:
+            counts_of(b, t)
+
+    finish1 = gather(win1, w1_send, w1_recv, field, early_counts, absorber(win1))
+    potential = -damping * entropy * reduce(count1)
+    sp_out[...] = potential
     eye = lax.broadcasted_iota(jnp.int32, (tiles, tiles), 0) == lax.broadcasted_iota(
         jnp.int32, (tiles, tiles), 1
     )
-    cell_count = jnp.sum(jnp.where(eye, cnt_ref[...].astype(f32), 0.0), axis=1, keepdims=True)
+    cell_count = jnp.sum(jnp.where(eye, cells[...].astype(f32), 0.0), axis=1, keepdims=True)
     active = lax.broadcasted_iota(jnp.int32, (tiles, width), 1).astype(f32) < cell_count
-    source_field = jnp.where(active, potential / entropy + jnp.log(sm_ref[...]), -jnp.inf)
-    finish2 = gather(win2, w2_send, w2_recv, source_field, lambda: None)
-    tp_ref[...] = -damping * entropy * reduce(win2, count2)
+    source_field = jnp.where(active, potential / entropy + jnp.log(fine[2]), -jnp.inf)
+    finish2 = gather(
+        win2, w2_send, w2_recv, source_field, late_counts, absorber(win2)
+    )
+    stores[2].start()
+    tp_out[...] = -damping * entropy * reduce(count2)
+    stores[3].start()
 
     for db, dt in around:
         when(there(db, dt), lambda db=db, dt=dt: coarse_copy(db, dt).wait_send())
@@ -425,6 +501,17 @@
         when(has_band[db], lambda db=db, k=k: pair_copy(db, k).wait_send())
     finish1()
     finish2()
+    for store in stores:
+        store.wait()
+
+
+def write_out(*refs):
+    sources, targets, sems = refs[0:4], refs[4:8], refs[8]
+    copies = [pltpu.make_async_copy(sources[i], targets[i], sems.at[i]) for i in range(4)]
+    for copy in copies:
+        copy.start()
+    for copy in copies:
+        copy.wait()
 
 
 def per_device(cs, ct, off, sm, tm, cnt, ps, pt):
@@ -432,29 +519,42 @@
     n_tile = lax.axis_size("tile")
     rows, cols = cs.shape
     tiles, width = off.shape
-    pair = jnp.concatenate([ps.reshape(-1, 128), pt.reshape(-1, 128)], axis=0)
     f32 = jnp.float32
+    slots = ps.shape[0]
     window = 3 * n_tile * tiles
     dma = pltpu.SemaphoreType.DMA
-    return pl.pallas_call(
+    shapes = (
+        jax.ShapeDtypeStruct((rows, cols), f32),
+        jax.ShapeDtypeStruct((rows, cols), f32),
+        jax.ShapeDtypeStruct((tiles, width), f32),
+        jax.ShapeDtypeStruct((tiles, width), f32),
+    )
+    results = pl.pallas_call(
         functools.partial(kernel, n_band, n_tile),
-        out_shape=(
-            jax.ShapeDtypeStruct((rows, cols), f32),
-            jax.ShapeDtypeStruct((rows, cols), f32),
-            jax.ShapeDtypeStruct((tiles, width), f32),
-            jax.ShapeDtypeStruct((tiles, width), f32),
-        ),
-        in_specs=[pl.BlockSpec(memory_space=pltpu.VMEM)] * 7,
-        out_specs=[pl.BlockSpec(memory_space=pltpu.VMEM)] * 4,
+        out_shape=shapes,
+        in_specs=[pl.BlockSpec(memory_space=pltpu.HBM)] * 8,
+        out_specs=[pl.BlockSpec(memory_space=pltpu.HBM)] * 4,
         scratch_shapes=[
-            pltpu.VMEM((3, 3, 2 * rows, cols), f32),
+            pltpu.VMEM((3, tiles, width), f32),
+            pltpu.VMEM((1, tiles), jnp.int32),
+            dma((8,)),
+            pltpu.VMEM((rows, cols), f32),
+            pltpu.VMEM((rows, cols), f32),
+            pltpu.VMEM((tiles, width), f32),
+            pltpu.VMEM((tiles, width), f32),
+            dma((4,)),
+            pltpu.VMEM((3, 2, rows, cols), f32),
+            pltpu.VMEM((3, 2, rows, cols), f32),
+            pltpu.VMEM((2, rows, cols), f32),
             pltpu.VMEM((2, 3 * rows, 2 * cols), f32),
-            pltpu.VMEM((3, n_tile) + pair.shape, jnp.int32),
+            pltpu.VMEM((3, n_tile, 2, 1, slots), jnp.int32),
             pltpu.VMEM((3, n_tile, tiles, width), f32),
             pltpu.VMEM((3, n_tile, tiles, width), f32),
             pltpu.VMEM((tiles, window), f32),
             pltpu.VMEM((tiles, window), f32),
-            pltpu.VMEM((n_tile, width, width), f32),
+            pltpu.VMEM((2 * width, 2 * width), jnp.bfloat16),
+            pltpu.VMEM((window, 2 * width), jnp.bfloat16),
+            pltpu.VMEM((1, window), f32),
             dma((3, 3)),
             dma((3, 3)),
             dma((3, n_tile)),
@@ -465,9 +565,17 @@
             dma((3, n_tile)),
         ],
         compiler_params=pltpu.CompilerParams(
-            collective_id=0, has_side_effects=True, vmem_limit_bytes=32 * 1024 * 1024
+            collective_id=0, has_side_effects=True, vmem_limit_bytes=60 * 1024 * 1024
         ),
-    )(cs, ct, off, sm, tm, cnt.reshape(1, tiles), pair)
+    )(cs, ct, off, sm, tm, cnt.reshape(1, tiles), ps.reshape(1, slots), pt.reshape(1, slots))
+    return pl.pallas_call(
+        write_out,
+        out_shape=shapes,
+        in_specs=[pl.BlockSpec(memory_space=pltpu.HBM)] * 4,
+        out_specs=[pl.BlockSpec(memory_space=pltpu.HBM)] * 4,
+        scratch_shapes=[dma((4,))],
+        compiler_params=pltpu.CompilerParams(vmem_limit_bytes=60 * 1024 * 1024),
+    )(*results)
 
 
 def solution(mesh):

time: 31.3 us -> 27.6 us (0.88); the launches traced: 30.7 us -> 27.4 us
  local copies, waits for them, and re-layouts: 5.26 us -> 0 us
  Pallas kernels: 24.1 us -> 26.7 us
  other arithmetic: 0.72 us -> 0 us
    unnamed x16 -> x0, local copies, waits for them, and re-layouts: 5.26 us -> none
    pallas_call x1 -> x2, Pallas kernels: 24.1 us -> 26.7 us  [the longest x1 24.1 us: per_device(): pl.pallas_call(functools.partial(kernel, n_band, n_tile), out_shape=shape...]
    concatenate x1 -> x0, other arithmetic: 0.72 us -> none  [per_device(): pair = jnp.concatenate([ps.reshape(-1, 128), pt.reshape(-1, 128)], axis=0)]
where the time goes in v2:
time: 27.6 us; the launch traced here: 27.4 us
  Pallas kernels  26.7 us (97%)
  between operations  0.64 us (2%)
    pallas_call x1, Pallas kernels, per_device(): pl.pallas_call(functools.partial(kernel, n_band, n_tile), out_shape=shape...  24.1 us
    pallas_call x1, Pallas kernels, per_device(): pl.pallas_call(write_out, out_shape=shapes, in_specs=[pl.BlockSpec(memory...  2.63 us

profile of v2, /device:TPU:3, one launch (start us, length us, event | category | flops | bytes accessed | tf_op | source)
XLA Modules:
  0.0 27.4 jit_solution(13425421413169966687)
XLA Ops:
  0.6 24.1 %shard_map.111 = (f32[16,128]{1,0:T(8,128)}, f32[16,128]{1,0:T(8,128)}, f32[32,128]{1,0:T(8,128)}, f32[32,128]{1,0:T(8,128)}) custom-call(f32[16,128]{1,0:T(8,128)} %cs_ref.1, f32[16,128]{1,0:T(8,128)} %ct_ref.1, f32[32,128]{1,0:T(8,128)} %off_ref.1, f32[32,128]{1,0:T(8,128)} %sm_ref.1, f32[32,128]{1,0:T(8,128)} %tm_ref.1, s32[1,32]{1,0:T(1,128)} %bitcast.5, ...), custom_call_target="tpu_custom_call" | custom-call | tf_op jit(solution)/shard_map/pallas_call | solution.py:532
  24.7 2.6 %shard_map.112 = (f32[16,128]{1,0:T(8,128)}, f32[16,128]{1,0:T(8,128)}, f32[32,128]{1,0:T(8,128)}, f32[32,128]{1,0:T(8,128)}) custom-call(f32[16,128]{1,0:T(8,128)} %get-tuple-element.8.refs_0_, f32[16,128]{1,0:T(8,128)} %get-tuple-element.9.refs_1_, f32[32,128]{1,0:T(8,128)} %get-tuple-element.10.refs_2_, f32[32,128]{1,0:T(8,128)} %get-tuple-element.11.refs_3_), custom_call_target="tpu_custom_call" | custom-call | tf_op jit(solution)/shard_map/pallas_call | solution.py:571

commit v3 on v2

--- a/solution.py
+++ b/solution.py
@@ -47,10 +47,7 @@
     cnt_ref,
     ps_ref,
     pt_ref,
-    u_ref,
-    v_ref,
-    sp_ref,
-    tp_ref,
+    out_ref,
     fine,
     cells,
     arrived,
@@ -91,6 +88,16 @@
     barrier = pltpu.get_barrier_semaphore()
     has_band = {-1: band > 0, 0: True, 1: band < n_band - 1}
 
+    odd = lax.rem(band, 2) == 1
+    paired = {
+        -1: jnp.logical_and(has_band[-1], odd),
+        1: jnp.logical_and(has_band[1], jnp.logical_not(odd)),
+    }
+    apart = {
+        -1: jnp.logical_and(has_band[-1], jnp.logical_not(odd)),
+        1: jnp.logical_and(has_band[1], odd),
+    }
+
     def when(cond, body):
         if cond is True:
             body()
@@ -131,7 +138,12 @@
     stores = [
         pltpu.make_async_copy(src, dst, stored.at[i])
         for i, (src, dst) in enumerate(
-            ((u_out, u_ref), (v_out, v_ref), (sp_out, sp_ref), (tp_out, tp_ref))
+            (
+                (u_out, out_ref.at[0:rows]),
+                (v_out, out_ref.at[rows : 2 * rows]),
+                (sp_out, out_ref.at[2 * rows : 2 * rows + tiles]),
+                (tp_out, out_ref.at[2 * rows + tiles : 2 * rows + 2 * tiles]),
+            )
         )
     ]
     for db in (-1, 1):
@@ -360,17 +372,17 @@
     def gather(win, send, recv, value, between, absorb):
         win[1, tile] = value
 
-        def over_tile(k):
+        def outward(db, k):
             return pltpu.make_async_remote_copy(
                 src_ref=win.at[1, tile],
-                dst_ref=win.at[1, tile],
-                send_sem=send.at[1, k],
-                recv_sem=recv.at[1, tile],
-                device_id=device(0, k),
+                dst_ref=win.at[1 - db, tile],
+                send_sem=send.at[1 + db, k],
+                recv_sem=recv.at[1 - db, tile],
+                device_id=device(db, k),
                 device_id_type=MESH,
             )
 
-        def over_band(db, k):
+        def onward(db, k):
             src = lax.rem(tile + k, n_tile)
             return pltpu.make_async_remote_copy(
                 src_ref=win.at[1, src],
@@ -384,24 +396,26 @@
         def arrive(db, k):
             src = lax.rem(tile + k, n_tile)
             return pltpu.make_async_remote_copy(
-                src_ref=win.at[1, src],
+                src_ref=win.at[1, tile],
                 dst_ref=win.at[1 + db, src],
                 send_sem=send.at[1 + db, k],
                 recv_sem=recv.at[1 + db, src],
-                device_id=device(db, 0) if db else device(0, k),
+                device_id=device(db, k),
                 device_id_type=MESH,
             )
 
         order = sorted(range(1, n_tile), key=lambda k: min(k, n_tile - k))
         for k in reversed(order):
-            over_tile(k).start()
-        for db in (-1, 1):
-            when(has_band[db], lambda db=db: over_band(db, 0).start())
-        between()
+            outward(0, k).start()
+        for k in list(reversed(order)) + [0]:
+            for db in (-1, 1):
+                go = apart[db] if k else has_band[db]
+                when(go, lambda db=db, k=k: outward(db, k).start())
         for k in order:
             arrive(0, k).wait_recv()
             for db in (-1, 1):
-                when(has_band[db], lambda db=db, k=k: over_band(db, k).start())
+                when(paired[db], lambda db=db, k=k: onward(db, k).start())
+        between()
         absorb(1)
         for db in (-1, 1):
 
@@ -413,15 +427,11 @@
             absorb(1 + db)
 
         def finish():
-            for k in order:
-                over_tile(k).wait_send()
-            for db in (-1, 1):
-
-                def sent(db=db):
-                    for k in range(n_tile):
-                        over_band(db, k).wait_send()
-
-                when(has_band[db], sent)
+            for db, k in partners:
+                go = apart[db] if db and k else has_band[db]
+                when(go, lambda db=db, k=k: outward(db, k).wait_send())
+                if db and k:
+                    when(paired[db], lambda db=db, k=k: onward(db, k).wait_send())
 
         return finish
 
@@ -505,13 +515,12 @@
         store.wait()
 
 
-def write_out(*refs):
-    sources, targets, sems = refs[0:4], refs[4:8], refs[8]
-    copies = [pltpu.make_async_copy(sources[i], targets[i], sems.at[i]) for i in range(4)]
-    for copy in copies:
-        copy.start()
-    for copy in copies:
-        copy.wait()
+def write_out(packed, *outs):
+    at = 0
+    for out in outs:
+        count = out.shape[0]
+        out[...] = packed[at : at + count]
+        at += count
 
 
 def per_device(cs, ct, off, sm, tm, cnt, ps, pt):
@@ -529,11 +538,11 @@
         jax.ShapeDtypeStruct((tiles, width), f32),
         jax.ShapeDtypeStruct((tiles, width), f32),
     )
-    results = pl.pallas_call(
+    packed = pl.pallas_call(
         functools.partial(kernel, n_band, n_tile),
-        out_shape=shapes,
+        out_shape=jax.ShapeDtypeStruct((2 * rows + 2 * tiles, width), f32),
         in_specs=[pl.BlockSpec(memory_space=pltpu.HBM)] * 8,
-        out_specs=[pl.BlockSpec(memory_space=pltpu.HBM)] * 4,
+        out_specs=pl.BlockSpec(memory_space=pltpu.HBM),
         scratch_shapes=[
             pltpu.VMEM((3, tiles, width), f32),
             pltpu.VMEM((1, tiles), jnp.int32),
@@ -571,11 +580,8 @@
     return pl.pallas_call(
         write_out,
         out_shape=shapes,
-        in_specs=[pl.BlockSpec(memory_space=pltpu.HBM)] * 4,
-        out_specs=[pl.BlockSpec(memory_space=pltpu.HBM)] * 4,
-        scratch_shapes=[dma((4,))],
         compiler_params=pltpu.CompilerParams(vmem_limit_bytes=60 * 1024 * 1024),
-    )(*results)
+    )(packed)
 
 
 def solution(mesh):

time: 27.6 us -> 24.7 us (0.89)
  Pallas kernels: 26.7 us -> 23.6 us
    pallas_call x2, Pallas kernels: 26.7 us -> 23.6 us  [the longest x1 22.2 us: per_device(): pl.pallas_call(functools.partial(kernel, n_band, n_tile), out_shape=jax.S...]
where the time goes in v3:
time: 24.7 us; the launch traced here: 24.3 us
  Pallas kernels  23.6 us (96%)
  between operations  0.64 us (3%)
    pallas_call x1, Pallas kernels, per_device(): pl.pallas_call(functools.partial(kernel, n_band, n_tile), out_shape=jax.S...  22.2 us
    pallas_call x1, Pallas kernels, per_device(): pl.pallas_call(write_out, out_shape=shapes, compiler_params=pltpu.Compile...  1.42 us

profile of v3, /device:TPU:3, one launch (start us, length us, event | category | flops | bytes accessed | tf_op | source)
XLA Modules:
  0.0 24.3 jit_solution(18092270138956516420)
XLA Ops:
  0.6 22.2 %shard_map.111.packed = f32[96,128]{1,0:T(8,128)} custom-call(f32[16,128]{1,0:T(8,128)} %cs_ref.1, f32[16,128]{1,0:T(8,128)} %ct_ref.1, f32[32,128]{1,0:T(8,128)} %off_ref.1, f32[32,128]{1,0:T(8,128)} %sm_ref.1, f32[32,128]{1,0:T(8,128)} %tm_ref.1, s32[1,32]{1,0:T(1,128)} %bitcast.5, s32[1,512]{1,0:T(1,128)} %bitcast.3, s32[1,512]{1,0:T(1,128)} %bitcast.4), custom_call_target="tpu_custom_call" | custom-call | tf_op jit(solution)/shard_map/pallas_call | solution.py:541
  22.9 1.4 %shard_map.112 = (f32[16,128]{1,0:T(8,128)}, f32[16,128]{1,0:T(8,128)}, f32[32,128]{1,0:T(8,128)}, f32[32,128]{1,0:T(8,128)}) custom-call(f32[96,128]{1,0:T(8,128)} %shard_map.111.packed), custom_call_target="tpu_custom_call" | custom-call | tf_op jit(solution)/shard_map/pallas_call | solution.py:580

commit v4 on v3

--- a/solution.py
+++ b/solution.py
@@ -405,9 +405,9 @@
             )
 
         order = sorted(range(1, n_tile), key=lambda k: min(k, n_tile - k))
-        for k in reversed(order):
+        for k in order:
             outward(0, k).start()
-        for k in list(reversed(order)) + [0]:
+        for k in [0] + order:
             for db in (-1, 1):
                 go = apart[db] if k else has_band[db]
                 when(go, lambda db=db, k=k: outward(db, k).start())

time: 24.7 us -> 24.4 us (0.988)
  no operation moved by 1% of the time
where the time goes in v4:
time: 24.4 us; the launch traced here: 24.1 us
  Pallas kernels  23.5 us (96%)
  between operations  0.64 us (3%)
    pallas_call x1, Pallas kernels, per_device(): pl.pallas_call(functools.partial(kernel, n_band, n_tile), out_shape=jax.S...  22 us
    pallas_call x1, Pallas kernels, per_device(): pl.pallas_call(write_out, out_shape=shapes, compiler_params=pltpu.Compile...  1.42 us

profile of v4, /device:TPU:3, one launch (start us, length us, event | category | flops | bytes accessed | tf_op | source)
XLA Modules:
  0.0 24.1 jit_solution(1620104955954260149)
XLA Ops:
  0.6 22.0 %shard_map.111.packed = f32[96,128]{1,0:T(8,128)} custom-call(f32[16,128]{1,0:T(8,128)} %cs_ref.1, f32[16,128]{1,0:T(8,128)} %ct_ref.1, f32[32,128]{1,0:T(8,128)} %off_ref.1, f32[32,128]{1,0:T(8,128)} %sm_ref.1, f32[32,128]{1,0:T(8,128)} %tm_ref.1, s32[1,32]{1,0:T(1,128)} %bitcast.5, s32[1,512]{1,0:T(1,128)} %bitcast.3, s32[1,512]{1,0:T(1,128)} %bitcast.4), custom_call_target="tpu_custom_call" | custom-call | tf_op jit(solution)/shard_map/pallas_call | solution.py:541
  22.7 1.4 %shard_map.112 = (f32[16,128]{1,0:T(8,128)}, f32[16,128]{1,0:T(8,128)}, f32[32,128]{1,0:T(8,128)}, f32[32,128]{1,0:T(8,128)}) custom-call(f32[96,128]{1,0:T(8,128)} %shard_map.111.packed), custom_call_target="tpu_custom_call" | custom-call | tf_op jit(solution)/shard_map/pallas_call | solution.py:580

commit v5 on v4

--- a/solution.py
+++ b/solution.py
@@ -206,7 +206,7 @@
             device_id_type=MESH,
         )
 
-    around = [(db, dt) for dt in (-1, 1, 0) for db in (-1, 0, 1) if (db, dt) != (0, 0)]
+    around = [(db, dt) for dt in (0, -1, 1) for db in (0, -1, 1) if (db, dt) != (0, 0)]
 
     def there(db, dt):
         ok = None

time: 24.4 us -> 24.6 us (level)
  no operation moved by 1% of the time
where the time goes in v5:
time: 24.6 us; the launch traced here: 24.2 us
  Pallas kernels  23.5 us (96%)
  between operations  0.64 us (3%)
    pallas_call x1, Pallas kernels, per_device(): pl.pallas_call(functools.partial(kernel, n_band, n_tile), out_shape=jax.S...  22.1 us
    pallas_call x1, Pallas kernels, per_device(): pl.pallas_call(write_out, out_shape=shapes, compiler_params=pltpu.Compile...  1.42 us

profile of v5, /device:TPU:3, one launch (start us, length us, event | category | flops | bytes accessed | tf_op | source)
XLA Modules:
  0.0 24.2 jit_solution(156198566012343070)
XLA Ops:
  0.6 22.1 %shard_map.111.packed = f32[96,128]{1,0:T(8,128)} custom-call(f32[16,128]{1,0:T(8,128)} %cs_ref.1, f32[16,128]{1,0:T(8,128)} %ct_ref.1, f32[32,128]{1,0:T(8,128)} %off_ref.1, f32[32,128]{1,0:T(8,128)} %sm_ref.1, f32[32,128]{1,0:T(8,128)} %tm_ref.1, s32[1,32]{1,0:T(1,128)} %bitcast.5, s32[1,512]{1,0:T(1,128)} %bitcast.3, s32[1,512]{1,0:T(1,128)} %bitcast.4), custom_call_target="tpu_custom_call" | custom-call | tf_op jit(solution)/shard_map/pallas_call | solution.py:541
  22.8 1.4 %shard_map.112 = (f32[16,128]{1,0:T(8,128)}, f32[16,128]{1,0:T(8,128)}, f32[32,128]{1,0:T(8,128)}, f32[32,128]{1,0:T(8,128)}) custom-call(f32[96,128]{1,0:T(8,128)} %shard_map.111.packed), custom_call_target="tpu_custom_call" | custom-call | tf_op jit(solution)/shard_map/pallas_call | solution.py:580
